TPU v7x, 32 devices: a whole 2x2x4 slice. The times are simulated.
32 devices in a mesh: dp: 4 (over y, core), seq: 8 (over z, x).
Axes of the slice: x: 2, y: 2, z: 4, core: 2. Of those that a mesh axis runs over, the one named last changes fastest.
Arguments:
- source_embed: bfloat16 [2, 4, 1024, 1024], P(None, 'dp', 'seq'), may hold values from -6 to 6
- target_embed: bfloat16 [2, 4, 1024, 1024], P(None, 'dp', 'seq'), may hold values from -6 to 6
- source_docs: int32 [2, 4, 1024], P(None, 'dp', 'seq'), may hold values from 0 to 2, as said below
- target_docs: int32 [2, 4, 1024], P(None, 'dp', 'seq'), may hold values from 0 to 2, as said below
- label_index: int32 [2, 4, 48], P(None, 'dp', 'seq'), may hold values from 0 to 1023, as said below
- label_token: int32 [2, 4, 48], P(None, 'dp', 'seq'), may hold values from 0 to 32767
- attend_in: bfloat16 [3, 3, 1024, 1024], P(None, None, ('dp', 'seq')), may hold values from -0.1875 to 0.1875
- attend_out: bfloat16 [3, 1024, 1024], P(None, ('dp', 'seq')), may hold values from -0.75 to 0.75
- feed_up: bfloat16 [2, 1024, 4096], P(None, ('dp', 'seq')), may hold values from -0.1875 to 0.1875
- feed_down: bfloat16 [2, 4096, 1024], P(None, ('dp', 'seq')), may hold values from -0.09375 to 0.09375
- norm_gain: bfloat16 [9, 1024], P(None, ('dp', 'seq')), may hold values from 0.25 to 1.75
- norm_bias: bfloat16 [9, 1024], P(None, ('dp', 'seq')), may hold values from -2.5 to 2.5
- vocab_table: bfloat16 [32768, 1024], P(('dp', 'seq')), may hold values from -0.1875 to 0.1875
Outputs:
- mean_loss: float32 [], replicated
- source_grad: float32 [2, 4, 1024, 1024], P(None, 'dp', 'seq')
- target_grad: float32 [2, 4, 1024, 1024], P(None, 'dp', 'seq')
- attend_in_grad: float32 [3, 3, 1024, 1024], P(None, None, ('dp', 'seq'))
- attend_out_grad: float32 [3, 1024, 1024], P(None, ('dp', 'seq'))
- feed_up_grad: float32 [2, 1024, 4096], P(None, ('dp', 'seq'))
- feed_down_grad: float32 [2, 4096, 1024], P(None, ('dp', 'seq'))
- norm_gain_grad: float32 [9, 1024], P(None, ('dp', 'seq'))
- norm_bias_grad: float32 [9, 1024], P(None, ('dp', 'seq'))
- vocab_table_grad: float32 [32768, 1024], P(('dp', 'seq'))
Inputs may be any that keep to these rules, and one draw needn't show every extreme that they name: `source_docs`: each row holds the documents 0, 1 and 2 in this order; document 0 ends within the first 128 positions, document 2 begins within the last 128 positions. `target_docs`: each row holds the documents 0, 1 and 2 in this order; document 0 ends within the first 128 positions, document 2 begins within the last 128 positions. `label_index`: entries k * 6 to (k + 1) * 6 - 1 of a row are distinct positions from k * 128 to (k + 1) * 128 - 1; the first and the last position of every row carry a label.
All inputs are finite; a program needn't handle non-finite values.
Results may differ from a plain program's by a relative error of at most 0.015.
Values may be sent and summed in bfloat16 or wider, within the bound.
No kernel may reach another device: no remote copies, remote signals or barrier semaphores. Data moves between devices by JAX's collectives and lax.ppermute only.
A program may use at most 448 MiB of HBM per device.

v0:
```python
import math

import jax
import jax.numpy as jnp
from jax import lax
from jax.sharding import PartitionSpec as P

HEADS = 16
HEAD = 64


EPSILON = 1e-05
MASK_VALUE = -1000000000.0


def merged(part, axis, combine):
    gathered = jax.tree.map(lambda a: lax.all_gather(a, axis), part)

    def take(source):
        return jax.tree.map(lambda a: lax.dynamic_index_in_dim(a, source, 0, False), gathered)

    return lax.fori_loop(
        1, lax.axis_size(axis), lambda source, state: combine(state, take(source)), take(0)
    )


def layer_norm(values, gain_row, bias_row):
    center = jnp.mean(values, axis=-1, keepdims=True)
    shifted = values - center
    spread = jnp.mean(shifted * shifted, axis=-1, keepdims=True)
    return shifted * lax.rsqrt(spread + EPSILON) * gain_row + bias_row


def norm_back(values, gain_row, bias_row, gradient):
    unused, pull = jax.vjp(layer_norm, values, gain_row, bias_row)
    return pull(gradient)


def product(left, right):
    return jnp.dot(left, right, preferred_element_type=jnp.float32)


def rows_inner(left, right):
    return lax.dot_general(
        left, right, (((0,), (0,)), ((), ())), preferred_element_type=jnp.float32
    )


def stacked_inner(left, right):
    return lax.dot_general(
        left, right, (((1,), (1,)), ((0,), (0,))), preferred_element_type=jnp.float32
    )


def by_transpose(left, right):
    return lax.dot_general(
        left, right, (((1,), (1,)), ((), ())), preferred_element_type=jnp.float32
    )


def split_heads(matrix):
    return matrix.reshape(matrix.shape[0], HEADS, HEAD)


def exact_gelu(values):
    return jax.nn.gelu(values, approximate=False)


def fetch_all(attend_in, attend_out, feed_up, feed_down, norm_gain, norm_bias):
    return (
        lax.all_gather(attend_in, ("dp", "seq"), axis=2, tiled=True),
        lax.all_gather(attend_out, ("dp", "seq"), axis=1, tiled=True),
        lax.all_gather(feed_up, ("dp", "seq"), axis=1, tiled=True),
        lax.all_gather(feed_down, ("dp", "seq"), axis=1, tiled=True),
        lax.all_gather(norm_gain, ("dp", "seq"), axis=1, tiled=True),
        lax.all_gather(norm_bias, ("dp", "seq"), axis=1, tiled=True),
    )


def merge_stats(earlier, later):
    joint_max = jnp.maximum(earlier[0], later[0])
    joint_sum = earlier[1] * jnp.exp(earlier[0] - joint_max) + later[1] * jnp.exp(
        later[0] - joint_max
    )
    return (joint_max, joint_sum, earlier[2] + later[2])


def masked_scores(queries, all_keys, key_mask):
    scores = jnp.einsum(
        "qhd,khd->hqk",
        split_heads(queries),
        split_heads(all_keys),
        preferred_element_type=jnp.float32,
    )
    return jnp.where(key_mask[None], scores * (1.0 / math.sqrt(HEAD)), MASK_VALUE)


def attend_forward(
    query_in, key_in, weight_in, weight_out, query_docs, key_docs, query_places, causal
):
    queries = product(query_in, weight_in[0]).astype(jnp.bfloat16)
    own_keys = product(key_in, weight_in[1]).astype(jnp.bfloat16)
    own_values = product(key_in, weight_in[2]).astype(jnp.bfloat16)
    all_keys, all_values, all_docs = (
        lax.all_gather(own_keys, "seq", axis=0, tiled=True),
        lax.all_gather(own_values, "seq", axis=0, tiled=True),
        lax.all_gather(key_docs.astype(jnp.bfloat16), "seq", axis=0, tiled=True),
    )
    key_places = jnp.arange(all_keys.shape[0])
    key_mask = query_docs[:, None] == all_docs.astype(jnp.int32)[None, :]
    if causal:
        key_mask = key_mask & (key_places[None, :] <= query_places[:, None])
    scores = masked_scores(queries, all_keys, key_mask)
    row_max = jnp.max(scores, axis=-1, keepdims=True)
    exponent = jnp.exp(scores - row_max)
    row_sum = jnp.sum(exponent, axis=-1, keepdims=True)
    attention = (exponent / row_sum).astype(jnp.bfloat16)
    mixed_heads = jnp.einsum(
        "hqk,khd->qhd", attention, split_heads(all_values), preferred_element_type=jnp.float32
    )
    mixed_heads = mixed_heads.reshape(queries.shape).astype(jnp.bfloat16)
    stored = (
        queries,
        all_keys,
        all_values,
        key_mask,
        row_max + jnp.log(row_sum),
        mixed_heads,
        query_docs,
        key_docs,
        query_places,
        causal,
    )
    return (product(mixed_heads, weight_out), stored)


def attend_backward(stored, query_in, key_in, weight_in, weight_out, gradient):
    (
        queries,
        all_keys,
        all_values,
        key_mask,
        log_total,
        mixed_heads,
        query_docs,
        key_docs,
        query_places,
        causal,
    ) = stored
    grad_branch = gradient.astype(jnp.bfloat16)
    grad_mixed = by_transpose(grad_branch, weight_out).astype(jnp.bfloat16)
    attention = jnp.exp(masked_scores(queries, all_keys, key_mask) - log_total)
    grad_attention = jnp.einsum(
        "qhd,khd->hqk",
        split_heads(grad_mixed),
        split_heads(all_values),
        preferred_element_type=jnp.float32,
    )
    row_delta = jnp.sum(attention * grad_attention, axis=-1, keepdims=True)
    grad_scores = (attention * (grad_attention - row_delta)).astype(jnp.bfloat16)
    score_scale = 1.0 / math.sqrt(HEAD)
    grad_queries = jnp.einsum(
        "hqk,khd->qhd", grad_scores, split_heads(all_keys), preferred_element_type=jnp.float32
    )
    grad_queries = (grad_queries * score_scale).reshape(queries.shape).astype(jnp.bfloat16)
    tokens = queries.shape[0]
    all_queries, all_grad_mixed = (
        lax.all_gather(queries, "seq", axis=0, tiled=True),
        lax.all_gather(grad_mixed, "seq", axis=0, tiled=True),
    )
    all_log, all_delta, all_query_docs = (
        lax.all_gather(log_total, "seq", axis=1, tiled=True),
        lax.all_gather(row_delta, "seq", axis=1, tiled=True),
        lax.all_gather(query_docs.astype(jnp.float32), "seq", axis=0, tiled=True),
    )
    own_start = lax.axis_index("seq") * tokens
    own_keys = lax.dynamic_slice_in_dim(all_keys, own_start, tokens, 0)
    own_values = lax.dynamic_slice_in_dim(all_values, own_start, tokens, 0)
    own_places = own_start + jnp.arange(tokens)
    every_place = jnp.arange(all_queries.shape[0])
    mask_turned = key_docs[:, None] == all_query_docs.astype(jnp.int32)[None, :]
    if causal:
        mask_turned = mask_turned & (own_places[:, None] <= every_place[None, :])
    scores_turned = jnp.einsum(
        "khd,qhd->hkq",
        split_heads(own_keys),
        split_heads(all_queries),
        preferred_element_type=jnp.float32,
    )
    scores_turned = jnp.where(mask_turned[None], scores_turned * score_scale, MASK_VALUE)
    attention_turned = jnp.exp(scores_turned - jnp.swapaxes(all_log, 1, 2))
    grad_attention_turned = jnp.einsum(
        "khd,qhd->hkq",
        split_heads(own_values),
        split_heads(all_grad_mixed),
        preferred_element_type=jnp.float32,
    )
    grad_scores_turned = (
        attention_turned * (grad_attention_turned - jnp.swapaxes(all_delta, 1, 2))
    ).astype(jnp.bfloat16)
    grad_keys = jnp.einsum(
        "hkq,qhd->khd",
        grad_scores_turned,
        split_heads(all_queries),
        preferred_element_type=jnp.float32,
    )
    grad_keys = (grad_keys * score_scale).reshape(own_keys.shape)
    grad_values = jnp.einsum(
        "hkq,qhd->khd",
        attention_turned.astype(jnp.bfloat16),
        split_heads(all_grad_mixed),
        preferred_element_type=jnp.float32,
    )
    grad_values = grad_values.reshape(own_values.shape)
    grad_keys = grad_keys.astype(jnp.bfloat16)
    grad_values = grad_values.astype(jnp.bfloat16)
    grad_query_in = by_transpose(grad_queries, weight_in[0])
    grad_key_in = by_transpose(grad_keys, weight_in[1]) + by_transpose(grad_values, weight_in[2])
    pieces = (query_in, grad_queries, key_in, grad_keys, grad_values, mixed_heads, grad_branch)
    return (grad_query_in, grad_key_in, pieces)


def feed_forward_local(residual, gain_row, bias_row, weight_up, weight_down):
    normed = layer_norm(residual, gain_row, bias_row).astype(jnp.bfloat16)
    up_proj = product(normed, weight_up)
    hidden = exact_gelu(up_proj).astype(jnp.bfloat16)
    return (product(hidden, weight_down), (normed, up_proj, hidden))


def feed_backward(stored, residual, gain_row, bias_row, weight_up, weight_down, gradient):
    normed, up_proj, hidden = stored
    grad_branch = gradient.astype(jnp.bfloat16)
    grad_hidden = by_transpose(grad_branch, weight_down)
    unused, gelu_pull = jax.vjp(exact_gelu, up_proj)
    grad_upward = gelu_pull(grad_hidden)[0].astype(jnp.bfloat16)
    grad_normed = by_transpose(grad_upward, weight_up)
    grad_residual, grad_gain, grad_bias = norm_back(residual, gain_row, bias_row, grad_normed)
    return (
        gradient + grad_residual,
        grad_gain,
        grad_bias,
        (normed, grad_upward, hidden, grad_branch),
    )


def local(
    source_embed,
    target_embed,
    source_docs,
    target_docs,
    label_index,
    label_token,
    attend_in,
    attend_out,
    feed_up,
    feed_down,
    norm_gain,
    norm_bias,
    vocab_table,
):
    micro = source_embed.shape[0]
    tokens = source_embed.shape[2]
    width = source_embed.shape[3]
    norms = norm_gain.shape[0]
    vocab_rows = vocab_table.shape[0]
    own_places = lax.axis_index("seq") * tokens + jnp.arange(tokens)
    vocab_places = lax.axis_index(("dp", "seq")) * vocab_rows + jnp.arange(vocab_rows)
    ledger = {
        "gains": jnp.zeros((norms, width), jnp.float32),
        "biases": jnp.zeros((norms, width), jnp.float32),
    }
    attn_pieces = {0: [], 1: [], 2: []}
    feed_pieces = {0: [], 1: []}

    def record_norm(which, grad_gain, grad_bias):
        ledger["gains"] = ledger["gains"].at[which].add(grad_gain)
        ledger["biases"] = ledger["biases"].at[which].add(grad_bias)

    every_token = lax.all_gather(label_token[:, 0], ("dp", "seq"), axis=1, tiled=True)
    loss_sum = jnp.zeros((), jnp.float32)
    label_count = 0
    table_grad = jnp.zeros(vocab_table.shape, jnp.float32)
    source_grads = []
    target_grads = []
    for micro_index in range(micro):
        weights = fetch_all(attend_in, attend_out, feed_up, feed_down, norm_gain, norm_bias)
        w_in, w_out, w_up, w_down, gain_all, bias_all = weights
        gains = gain_all.astype(jnp.float32)
        biases = bias_all.astype(jnp.float32)
        source = source_embed[micro_index, 0].astype(jnp.float32)
        target = target_embed[micro_index, 0].astype(jnp.float32)
        source_row_docs = source_docs[micro_index, 0]
        target_row_docs = target_docs[micro_index, 0]
        enc_start = layer_norm(source, gains[0], biases[0])
        enc_normed = layer_norm(enc_start, gains[1], biases[1]).astype(jnp.bfloat16)
        enc_branch, enc_stored = attend_forward(
            enc_normed,
            enc_normed,
            w_in[0],
            w_out[0],
            source_row_docs,
            source_row_docs,
            own_places,
            False,
        )
        enc_middle = enc_start + enc_branch
        enc_feed_branch, enc_feed_stored = feed_forward_local(
            enc_middle, gains[2], biases[2], w_up[0], w_down[0]
        )
        enc_end = enc_middle + enc_feed_branch
        encoded = layer_norm(enc_end, gains[3], biases[3]).astype(jnp.bfloat16)
        dec_start = layer_norm(target, gains[4], biases[4])
        dec_normed = layer_norm(dec_start, gains[5], biases[5]).astype(jnp.bfloat16)
        self_branch, self_stored = attend_forward(
            dec_normed,
            dec_normed,
            w_in[1],
            w_out[1],
            target_row_docs,
            target_row_docs,
            own_places,
            True,
        )
        dec_self = dec_start + self_branch
        cross_normed = layer_norm(dec_self, gains[6], biases[6]).astype(jnp.bfloat16)
        cross_branch, cross_stored = attend_forward(
            cross_normed,
            encoded,
            w_in[2],
            w_out[2],
            target_row_docs,
            source_row_docs,
            own_places,
            False,
        )
        dec_cross = dec_self + cross_branch
        dec_feed_branch, dec_feed_stored = feed_forward_local(
            dec_cross, gains[7], biases[7], w_up[1], w_down[1]
        )
        dec_end = dec_cross + dec_feed_branch
        final = layer_norm(dec_end, gains[8], biases[8])
        local_index = label_index[micro_index, 0] - lax.axis_index("seq") * tokens
        picked_rows = jnp.take(final, local_index, axis=0).astype(jnp.bfloat16)
        all_rows = lax.all_gather(picked_rows, ("dp", "seq"), axis=0, tiled=True)
        all_tokens = every_token[micro_index]
        logits = by_transpose(all_rows, vocab_table)
        target_hit = all_tokens[:, None] == vocab_places[None, :]
        row_max = jnp.max(logits, axis=-1)
        row_sum = jnp.sum(jnp.exp(logits - row_max[:, None]), axis=-1)
        target_logit = jnp.sum(jnp.where(target_hit, logits, 0.0), axis=-1)
        row_max, row_sum, target_logit = merged(
            (row_max, row_sum, target_logit), ("dp", "seq"), merge_stats
        )
        log_total = row_max + jnp.log(row_sum)
        loss_sum = loss_sum + jnp.sum(log_total - target_logit)
        label_count = label_count + all_rows.shape[0]
        grad_logits = (
            jnp.exp(logits - log_total[:, None]) - target_hit.astype(jnp.float32)
        ).astype(jnp.bfloat16)
        table_grad = table_grad + rows_inner(grad_logits, all_rows)
        grad_picked = lax.psum_scatter(
            product(grad_logits, vocab_table), ("dp", "seq"), scatter_dimension=0, tiled=True
        )
        grad_final = jnp.zeros((tokens, width), jnp.float32).at[local_index].add(grad_picked)
        grad_dec_end, grad_gain, grad_bias = norm_back(dec_end, gains[8], biases[8], grad_final)
        record_norm(8, grad_gain, grad_bias)
        grad_dec_cross, grad_gain, grad_bias, pieces = feed_backward(
            dec_feed_stored, dec_cross, gains[7], biases[7], w_up[1], w_down[1], grad_dec_end
        )
        record_norm(7, grad_gain, grad_bias)
        feed_pieces[1].append(pieces)
        grad_query_in, grad_encoded, pieces = attend_backward(
            cross_stored, cross_normed, encoded, w_in[2], w_out[2], grad_dec_cross
        )
        grad_part, grad_gain, grad_bias = norm_back(dec_self, gains[6], biases[6], grad_query_in)
        record_norm(6, grad_gain, grad_bias)
        grad_dec_self = grad_dec_cross + grad_part
        attn_pieces[2].append(pieces)
        grad_query_in, grad_key_in, pieces = attend_backward(
            self_stored, dec_normed, dec_normed, w_in[1], w_out[1], grad_dec_self
        )
        grad_part, grad_gain, grad_bias = norm_back(
            dec_start, gains[5], biases[5], grad_query_in + grad_key_in
        )
        record_norm(5, grad_gain, grad_bias)
        grad_dec_start = grad_dec_self + grad_part
        grad_target, grad_gain, grad_bias = norm_back(target, gains[4], biases[4], grad_dec_start)
        record_norm(4, grad_gain, grad_bias)
        attn_pieces[1].append(pieces)
        grad_enc_end, grad_gain, grad_bias = norm_back(enc_end, gains[3], biases[3], grad_encoded)
        record_norm(3, grad_gain, grad_bias)
        grad_enc_middle, grad_gain, grad_bias, pieces = feed_backward(
            enc_feed_stored, enc_middle, gains[2], biases[2], w_up[0], w_down[0], grad_enc_end
        )
        record_norm(2, grad_gain, grad_bias)
        feed_pieces[0].append(pieces)
        grad_query_in, grad_key_in, pieces = attend_backward(
            enc_stored, enc_normed, enc_normed, w_in[0], w_out[0], grad_enc_middle
        )
        grad_part, grad_gain, grad_bias = norm_back(
            enc_start, gains[1], biases[1], grad_query_in + grad_key_in
        )
        record_norm(1, grad_gain, grad_bias)
        grad_enc_start = grad_enc_middle + grad_part
        grad_source, grad_gain, grad_bias = norm_back(source, gains[0], biases[0], grad_enc_start)
        record_norm(0, grad_gain, grad_bias)
        attn_pieces[0].append(pieces)
        source_grads.append(grad_source)
        target_grads.append(grad_target)

    def attn_rows(sublayer, member):
        return jnp.concatenate([entry[member] for entry in attn_pieces[sublayer]], axis=0)

    def feed_rows(sublayer, member):
        return jnp.concatenate([entry[member] for entry in feed_pieces[sublayer]], axis=0)

    in_left = jnp.stack([attn_rows(sub, member) for sub in range(3) for member in (0, 2, 2)])
    in_right = jnp.stack([attn_rows(sub, member) for sub in range(3) for member in (1, 3, 4)])
    whole_in = stacked_inner(in_left, in_right).reshape(3, 3, width, width)
    whole_out = stacked_inner(
        jnp.stack([attn_rows(sub, 5) for sub in range(3)]),
        jnp.stack([attn_rows(sub, 6) for sub in range(3)]),
    )
    whole_up = stacked_inner(
        jnp.stack([feed_rows(sub, 0) for sub in range(2)]),
        jnp.stack([feed_rows(sub, 1) for sub in range(2)]),
    )
    whole_down = stacked_inner(
        jnp.stack([feed_rows(sub, 2) for sub in range(2)]),
        jnp.stack([feed_rows(sub, 3) for sub in range(2)]),
    )
    settled = (
        lax.psum_scatter(whole_in, ("dp", "seq"), scatter_dimension=2, tiled=True),
        lax.psum_scatter(whole_out, ("dp", "seq"), scatter_dimension=1, tiled=True),
        lax.psum_scatter(whole_up, ("dp", "seq"), scatter_dimension=1, tiled=True),
        lax.psum_scatter(whole_down, ("dp", "seq"), scatter_dimension=1, tiled=True),
        lax.psum_scatter(ledger["gains"], ("dp", "seq"), scatter_dimension=1, tiled=True),
        lax.psum_scatter(ledger["biases"], ("dp", "seq"), scatter_dimension=1, tiled=True),
    )
    mean_loss = loss_sum / label_count
    source_grad = jnp.stack(source_grads)[:, None]
    target_grad = jnp.stack(target_grads)[:, None]
    return (
        mean_loss,
        source_grad,
        target_grad,
        settled[0],
        settled[1],
        settled[2],
        settled[3],
        settled[4],
        settled[5],
        table_grad,
    )


def solution(mesh):
    placed = (
        P(None, "dp", "seq", None),
        P(None, "dp", "seq", None),
        P(None, "dp", "seq"),
        P(None, "dp", "seq"),
        P(None, "dp", "seq"),
        P(None, "dp", "seq"),
        P(None, None, ("dp", "seq"), None),
        P(None, ("dp", "seq"), None),
        P(None, ("dp", "seq"), None),
        P(None, ("dp", "seq"), None),
        P(None, ("dp", "seq")),
        P(None, ("dp", "seq")),
        P(("dp", "seq"), None),
    )
    return jax.shard_map(
        local,
        mesh=mesh,
        in_specs=placed,
        out_specs=(
            P(),
            P(None, "dp", "seq", None),
            P(None, "dp", "seq", None),
            P(None, None, ("dp", "seq"), None),
            P(None, ("dp", "seq"), None),
            P(None, ("dp", "seq"), None),
            P(None, ("dp", "seq"), None),
            P(None, ("dp", "seq")),
            P(None, ("dp", "seq")),
            P(("dp", "seq"), None),
        ),
        check_vma=False,
    )
```

profile of v0, /device:TPU:8, one launch (start us, length us, event | category | flops | bytes accessed | tf_op | source)
XLA Modules:
  0.0 5352.1 jit_solution(577273316552810393)
XLA Ops:
  8.0 67.9 %all-gather.19 = bf16[32,32,9]{1,2,0:T(8,128)(2,1)S(1)} all-gather(bf16[1,32,9]{1,2,0:T(8,128)(2,1)} %bitcast.1194), channel_id=1, replica_groups=mesh['dp'=4,'seq'=8] {'dp','seq'}, dimensions={0}, use_global_device_ids=true | all-gather | bytes 19008 | tf_op jit(solution)/shard_map/all_gather | solution.py:75
  76.0 66.3 %all-gather.20 = bf16[32,32,9]{1,2,0:T(8,128)(2,1)S(1)} all-gather(bf16[1,32,9]{1,2,0:T(8,128)(2,1)} %bitcast.1195), channel_id=1, replica_groups=mesh['dp'=4,'seq'=8] {'dp','seq'}, dimensions={0}, use_global_device_ids=true | all-gather | bytes 19008 | tf_op jit(solution)/shard_map/all_gather | solution.py:76
  383.9 37.6 all-gather.84.cloned.1.call-done
  436.4 100.3 %all-gather.72.cloned.1.call-done = bf16[2,1024,4096]{2,1,0:T(8,128)(2,1)} async-done(((bf16[2,32,4096]{2,1,0:T(8,128)(2,1)}), bf16[2,1024,4096]{2,1,0:T(8,128)(2,1)}) %all-gather.72.cloned.1.call-update) | async-done | bytes 16777232 | tf_op jit(solution)/shard_map/all_gather | solution.py:73
  545.7 107.0 %all-gather.74.cloned.1.call-done = bf16[2,4096,1024]{2,1,0:T(8,128)(2,1)} async-done(((bf16[2,128,1024]{2,1,0:T(8,128)(2,1)}), bf16[2,4096,1024]{2,1,0:T(8,128)(2,1)}) %all-gather.74.cloned.1.call-update) | async-done | bytes 16777232 | tf_op jit(solution)/shard_map/all_gather | solution.py:74
  688.3 65.3 %all-gather.2 = s32[2,1,192]{0,1,2:T(1,128)S(1)} all-gather(s32[2,1,6]{0,1,2:T(1,128)S(1)} %copy.332), channel_id=4, replica_groups=mesh['dp'=4,'seq'=8] {'dp','seq'}, dimensions={2}, use_global_device_ids=true | all-gather | bytes 1584 | tf_op jit(solution)/shard_map/all_gather | solution.py:279
  815.8 39.4 all-gather.80.cloned.1.call-done
  917.8 37.7 all-gather.76.cloned.1.call-done
  968.4 36.9 all-gather.90.cloned.1.call-done
  1018.4 36.7 all-gather.88.cloned.1.call-done
  1094.7 68.6 %all-gather.26 = bf16[32,6,1024]{2,1,0:T(8,128)(2,1)S(1)} all-gather(bf16[1,6,1024]{2,1,0:T(8,128)(2,1)S(1)} %fusion.410), channel_id=1, replica_groups=mesh['dp'=4,'seq'=8] {'dp','seq'}, dimensions={0}, use_global_device_ids=true | all-gather | bytes 405504 | tf_op jit(solution)/shard_map/all_gather | solution.py:344
  1165.6 68.5 %all-gather.23 = bf16[32,6,1024]{2,1,0:T(8,128)(2,1)S(1)} all-gather(bf16[1,6,1024]{2,1,0:T(8,128)(2,1)S(1)} %fusion.409), channel_id=1, replica_groups=mesh['dp'=4,'seq'=8] {'dp','seq'}, dimensions={0}, use_global_device_ids=true | all-gather | bytes 405504 | tf_op jit(solution)/shard_map/all_gather | solution.py:344
  1307.2 88.2 %all-reduce.16.cloned.1.call-done = (f32[6144]{0:T(1024)}, f32[6144]{0:T(1024)}, f32[6144]{0:T(1024)}, f32[6144]{0:T(1024)}, f32[6144]{0:T(1024)}, /*index=5*/f32[6144]{0:T(1024)}) async-done(((f32[6144]{0:T(1024)}, f32[6144]{0:T(1024)}, f32[6144]{0:T(1024)}, f32[6144]{0:T(1024)}, f32[6144]{0:T(1024)}, /*index=5*/f32[6144]{0:T(1024)}), (f32[6144]{0:T(1024)}, f32[6144]{0:T(1024)}, f32[6144]{0:T(1024)}, ...) | async-done | bytes 147472
  1411.4 121.6 %while.74 = (s32[]{:T(128)}, f32[192]{0:T(256)}, f32[192]{0:T(256)}, f32[192]{0:T(256)}, f32[32,192]{1,0:T(8,128)}, /*index=5*/f32[32,192]{1,0:T(8,128)}, f32[32,192]{1,0:T(8,128)}, s32[]{:T(128)}, s32[]{:T(128)}, s32[]{:T(128)}) while((s32[]{:T(128)}, f32[192]{0:T(256)}, f32[192]{0:T(256)}, f32[192]{0:T(256)}, f32[32,192]{1,0:T(8,128)}, ...), condition=%wide.region_28.30_spmd, body=%wide.region_27.29_spmd.sunk | while | flops 1349 | bytes 11671 | solution.py:22
  1533.0 121.7 %while.75 = (s32[]{:T(128)}, f32[192]{0:T(256)}, f32[192]{0:T(256)}, f32[192]{0:T(256)}, f32[32,192]{1,0:T(8,128)}, /*index=5*/f32[32,192]{1,0:T(8,128)}, f32[32,192]{1,0:T(8,128)}, s32[]{:T(128)}, s32[]{:T(128)}, s32[]{:T(128)}) while((s32[]{:T(128)}, f32[192]{0:T(256)}, f32[192]{0:T(256)}, f32[192]{0:T(256)}, f32[32,192]{1,0:T(8,128)}, ...), condition=%wide.region_58.60_spmd, body=%wide.region_57.59_spmd.sunk | while | flops 1349 | bytes 11671 | solution.py:22
  1662.3 77.9 %fusion.503 = (f32[8,1024]{1,0:T(8,128)S(1)}, f32[8,1024]{1,0:T(8,128)S(1)}) fusion(f32[192,1024]{1,0:T(8,128)} %fusion.485, f32[192,1024]{1,0:T(8,128)} %fusion.489), kind=kCustom, calls=%all-reduce-scatter.2 | all-reduce-scatter fusion | flops 524289 | bytes 1638400
  1822.7 30.8 all-gather.17
  1853.6 32.6 all-gather.9
  1924.9 32.6 all-gather.13
  1975.7 32.5 all-gather.11
  2009.5 32.5 all-gather.7
  2100.6 30.5 all-gather.12
  2131.0 32.5 all-gather.8
  2169.4 33.0 all-gather.16
  2208.0 32.0 all-gather.18
  2432.4 32.1 all-gather.10
  2464.5 32.9 all-gather.14
  2727.5 131.1 %reduce-scatter.23.cloned.1.call-done = f32[32,9]{1,0:T(8,128)} async-done(((f32[1024,9]{1,0:T(8,128)}), f32[32,9]{1,0:T(8,128)}) %reduce-scatter.23.cloned.1.call-update) | async-done | bytes 1168
  2860.0 271.0 %reduce-scatter.17.cloned.1.call-done = f32[3,32,1024]{2,1,0:T(8,128)} async-done(((f32[3,1024,1024]{2,1,0:T(8,128)}), f32[3,32,1024]{2,1,0:T(8,128)}) %reduce-scatter.17.cloned.1.call-update) | async-done | bytes 393232 | tf_op jit(solution)/shard_map/reduce_scatter | solution.py:434
  3131.0 708.5 %reduce-scatter.21.cloned.1.call-done = f32[2,128,1024]{2,1,0:T(8,128)} async-done(((f32[2,4096,1024]{2,1,0:T(8,128)}), f32[2,128,1024]{2,1,0:T(8,128)}) %reduce-scatter.21.cloned.1.call-update) | async-done | bytes 1048592 | tf_op jit(solution)/shard_map/reduce_scatter | solution.py:436
  3839.5 708.8 %reduce-scatter.19.cloned.1.call-done = f32[2,32,4096]{2,1,0:T(8,128)} async-done(((f32[2,1024,4096]{2,1,0:T(8,128)}), f32[2,32,4096]{2,1,0:T(8,128)}) %reduce-scatter.19.cloned.1.call-update) | async-done | bytes 1048592 | tf_op jit(solution)/shard_map/reduce_scatter | solution.py:435
  4548.3 796.0 %reduce-scatter.15.cloned.1.call-done = f32[3,3,32,1024]{3,2,1,0:T(8,128)} async-done(((f32[3,3,1024,1024]{3,2,1,0:T(8,128)}), f32[3,3,32,1024]{3,2,1,0:T(8,128)}) %reduce-scatter.15.cloned.1.call-update) | async-done | bytes 1179664 | tf_op jit(solution)/shard_map/reduce_scatter | solution.py:433
  (1828 shorter events, 1460.2 us)
Async XLA Ops:
  7.9 320.5 %all-gather.70.cloned.1.call-start = ((), (), s32[]{:S(2)}) async-start(), calls=%async_computation.11 | async-start | bytes 2359296 | tf_op jit(solution)/shard_map/all_gather | solution.py:105
  151.6 201.5 %all-gather.66.cloned.1.call-start = ((), (), s32[]{:S(2)}) async-start(), calls=%async_computation.9 | async-start | bytes 6488064 | tf_op jit(solution)/shard_map/all_gather | solution.py:72
  152.1 218.9 %all-gather.86.cloned.1.call-start = ((), (), s32[]{:S(2)}) async-start(), calls=%async_computation.19 | async-start | bytes 2359296 | tf_op jit(solution)/shard_map/all_gather | solution.py:105
  155.1 266.3 %all-gather.84.cloned.1.call-start = ((), (), s32[]{:S(2)}) async-start(), calls=%async_computation.18 | async-start | bytes 2359296 | tf_op jit(solution)/shard_map/all_gather | solution.py:106
  158.2 378.5 %all-gather.72.cloned.1.call-start = ((), (), s32[]{:S(2)}) async-start(), calls=%async_computation.12 | async-start | bytes 17301504 | tf_op jit(solution)/shard_map/all_gather | solution.py:73
  158.9 493.8 %all-gather.74.cloned.1.call-start = ((), (), s32[]{:S(2)}) async-start(), calls=%async_computation.13 | async-start | bytes 17301504 | tf_op jit(solution)/shard_map/all_gather | solution.py:74
  159.7 607.1 %all-gather.64.cloned.1.call-start = ((), (), s32[]{:S(2)}) async-start(), calls=%async_computation.8 | async-start | bytes 2359296 | tf_op jit(solution)/shard_map/all_gather | solution.py:105
  164.5 612.9 %all-gather.62.cloned.1.call-start = ((), (), s32[]{:S(2)}) async-start(), calls=%async_computation.7 | async-start | bytes 2359296 | tf_op jit(solution)/shard_map/all_gather | solution.py:106
  167.5 637.2 %all-gather.82.cloned.1.call-start = ((), (), s32[]{:S(2)}) async-start(), calls=%async_computation.17 | async-start | bytes 2359296 | tf_op jit(solution)/shard_map/all_gather | solution.py:105
  170.6 684.7 %all-gather.80.cloned.1.call-start = ((), (), s32[]{:S(2)}) async-start(), calls=%async_computation.16 | async-start | bytes 2359296 | tf_op jit(solution)/shard_map/all_gather | solution.py:106
  328.2 577.0 %all-gather.78.cloned.1.call-start = ((), (), s32[]{:S(2)}) async-start(), calls=%async_computation.15 | async-start | bytes 2359296 | tf_op jit(solution)/shard_map/all_gather | solution.py:105
  672.7 282.8 %all-gather.76.cloned.1.call-start = ((), (), s32[]{:S(2)}) async-start(), calls=%async_computation.14 | async-start | bytes 2359296 | tf_op jit(solution)/shard_map/all_gather | solution.py:106
  675.6 329.7 %all-gather.90.cloned.1.call-start = ((), (), s32[]{:S(2)}) async-start(), calls=%async_computation.21 | async-start | bytes 2359296 | tf_op jit(solution)/shard_map/all_gather | solution.py:105
  678.4 376.7 %all-gather.88.cloned.1.call-start = ((), (), s32[]{:S(2)}) async-start(), calls=%async_computation.20 | async-start | bytes 2359296 | tf_op jit(solution)/shard_map/all_gather | solution.py:106
  681.3 583.1 %all-gather.108.cloned.1.call-start = ((), (), s32[]{:S(2)}) async-start(), calls=%async_computation.30 | async-start | bytes 2359296 | tf_op jit(solution)/shard_map/all_gather | solution.py:168
  684.4 590.3 %all-gather.112.cloned.1.call-start = ((), (), s32[]{:S(2)}) async-start(), calls=%async_computation.32 | async-start | bytes 2359296 | tf_op jit(solution)/shard_map/all_gather | solution.py:168
  687.4 597.6 %all-gather.96.cloned.1.call-start = ((), (), s32[]{:S(2)}) async-start(), calls=%async_computation.24 | async-start | bytes 2359296 | tf_op jit(solution)/shard_map/all_gather | solution.py:168
  688.1 607.1 %all-gather.104.cloned.1.call-start = ((), (), s32[]{:S(2)}) async-start(), calls=%async_computation.28 | async-start | bytes 2359296 | tf_op jit(solution)/shard_map/all_gather | solution.py:168
  765.5 629.8 %all-reduce.16.cloned.1.call-start = ((), (), s32[]{:S(2)}) async-start(), calls=%async_computation.40 | async-start | bytes 294912
  1255.4 712.1 %all-gather.100.cloned.1.call-start = ((), (), s32[]{:S(2)}) async-start(), calls=%async_computation.26 | async-start | bytes 2359296 | tf_op jit(solution)/shard_map/all_gather | solution.py:168
  1257.4 714.0 %all-gather.92.cloned.1.call-start = ((), (), s32[]{:S(2)}) async-start(), calls=%async_computation.22 | async-start | bytes 2359296 | tf_op jit(solution)/shard_map/all_gather | solution.py:168
  1853.5 407.6 %all-gather.102.cloned.1.call-start = ((), (), s32[]{:S(2)}) async-start(), calls=%async_computation.27 | async-start | bytes 2359296 | tf_op jit(solution)/shard_map/all_gather | solution.py:169
  1924.9 355.0 %all-gather.94.cloned.1.call-start = ((), (), s32[]{:S(2)}) async-start(), calls=%async_computation.23 | async-start | bytes 2359296 | tf_op jit(solution)/shard_map/all_gather | solution.py:169
  2070.5 274.6 %all-gather.110.cloned.1.call-start = ((), (), s32[]{:S(2)}) async-start(), calls=%async_computation.31 | async-start | bytes 2359296 | tf_op jit(solution)/shard_map/all_gather | solution.py:169
  2096.6 268.4 %all-gather.114.cloned.1.call-start = ((), (), s32[]{:S(2)}) async-start(), calls=%async_computation.33 | async-start | bytes 2359296 | tf_op jit(solution)/shard_map/all_gather | solution.py:169
  2244.9 268.2 %all-gather.98.cloned.1.call-start = ((), (), s32[]{:S(2)}) async-start(), calls=%async_computation.25 | async-start | bytes 2359296 | tf_op jit(solution)/shard_map/all_gather | solution.py:169
  2411.7 314.4 %reduce-scatter.25.cloned.1.call-start = ((), (), s32[]{:S(2)}) async-start(), calls=%async_computation.39 | async-start | bytes 540672
  2593.1 265.5 %reduce-scatter.23.cloned.1.call-start = ((), (), s32[]{:S(2)}) async-start(), calls=%async_computation.38 | async-start | bytes 540672
  2602.1 528.8 %reduce-scatter.17.cloned.1.call-start = ((), (), s32[]{:S(2)}) async-start(), calls=%async_computation.35 | async-start | bytes 12976128 | tf_op jit(solution)/shard_map/reduce_scatter | solution.py:434
  2609.9 1229.6 %reduce-scatter.21.cloned.1.call-start = ((), (), s32[]{:S(2)}) async-start(), calls=%async_computation.37 | async-start | bytes 34603008 | tf_op jit(solution)/shard_map/reduce_scatter | solution.py:436
  2631.0 1917.3 %reduce-scatter.19.cloned.1.call-start = ((), (), s32[]{:S(2)}) async-start(), calls=%async_computation.36 | async-start | bytes 34603008 | tf_op jit(solution)/shard_map/reduce_scatter | solution.py:435
  2648.8 2695.4 %reduce-scatter.15.cloned.1.call-start = ((), (), s32[]{:S(2)}) async-start(), calls=%async_computation.34 | async-start | bytes 38928384 | tf_op jit(solution)/shard_map/reduce_scatter | solution.py:433
  (490 other events, 15259.1 us)
Sparse Core Ops, SparseCore 0:
  11.1 126.8 all-gather.59
  148.7 50.1 all-gather.69
  201.6 48.0 all-gather.67
  252.6 68.0 all-gather.65
  323.2 47.8 all-gather.85
  373.6 47.7 all-gather.83
  424.5 112.1 all-gather.71
  539.7 112.9 all-gather.73
  654.8 48.9 all-gather.63
  705.8 48.2 all-gather.61
  756.8 47.8 all-gather.81
  807.2 47.9 all-gather.79
  1007.3 47.7 all-gather.87
  1057.1 48.2 all-gather.107
  1108.0 51.0 all-gather.111
  1161.2 51.7 all-gather.95
  1215.0 49.1 all-gather.103
  1270.6 124.7 all-reduce.15
  1398.1 49.1 all-gather.99
  1853.6 50.1 all-gather.91
  1925.0 50.7 all-gather.101
  2070.6 51.0 all-gather.93
  2123.7 48.1 all-gather.109
  2245.0 50.5 all-gather.113
  2341.6 50.5 all-gather.97
  2411.8 50.6 all-gather.105
  2593.2 132.8 reduce-scatter.24
  2728.4 130.0 reduce-scatter.22
  2861.4 269.4 reduce-scatter.16
  3133.7 705.7 reduce-scatter.20
  3842.3 705.8 reduce-scatter.18
  4551.1 793.0 reduce-scatter.14
  (3 shorter events, 143.1 us)
where the time goes:
time: 5380 us; the launch traced here: 5350 us
  waiting for transfers between devices  3170 us (59%)
  blocking collectives  936 us (17%)
  matrix products  566 us (11%)
  local copies, waits for them, and re-layouts  339 us (6%)
  other arithmetic  267 us (5%)
    reduce_scatter x1, waiting for transfers between devices, local(): lax.psum_scatter(whole_in, ('dp', 'seq'), scatter_dimension=2, tiled=True)  796 us
    reduce_scatter x1, waiting for transfers between devices, local(): lax.psum_scatter(whole_up, ('dp', 'seq'), scatter_dimension=1, tiled=True)  709 us
    reduce_scatter x1, waiting for transfers between devices, local(): lax.psum_scatter(whole_down, ('dp', 'seq'), scatter_dimension=1, tiled=True)  708 us
    reduce_scatter x1, waiting for transfers between devices, local(): lax.psum_scatter(whole_out, ('dp', 'seq'), scatter_dimension=1, tiled=True)  271 us
    unnamed x54, waiting for transfers between devices  241 us
    all_gather x6, blocking collectives, attend_backward(): lax.all_gather(row_delta, 'seq', axis=1, tiled=True)  193 us
    all_gather x6, blocking collectives, attend_backward(): lax.all_gather(log_total, 'seq', axis=1, tiled=True)  190 us
    all_gather x6, waiting for transfers between devices, attend_forward(): lax.all_gather(own_values, 'seq', axis=0, tiled=True)  151 us
  transfers between devices with their start and end apart: 51, of which 17 were waited for; matrix products, arithmetic and copies ran while one was open for 22% of the time, Pallas kernels for 0%

commit v1 on v0

v1 whole, which is shorter than its diff:
```python
import functools
import math

import jax
import jax.numpy as jnp
from jax import lax
from jax.experimental import pallas as pl
from jax.experimental.pallas import tpu as pltpu
from jax.sharding import PartitionSpec as P

HEADS = 16
HEAD = 64

EPSILON = 1e-05
MASK_VALUE = -1000000000.0
AXES = ("r", "c", "a", "i", "b")
MEMBERS = ("c", "i")
BF16 = jnp.bfloat16
F32 = jnp.float32


def product(left, right):
    return jnp.dot(left, right, preferred_element_type=F32)


def by_transpose(left, right):
    return lax.dot_general(left, right, (((1,), (1,)), ((), ())), preferred_element_type=F32)


def rows_inner(left, right):
    return lax.dot_general(left, right, (((0,), (0,)), ((), ())), preferred_element_type=F32)


def tie(value, *others):
    return lax.optimization_barrier((value,) + others)[0]


class Grid:
    def __init__(self, dp, seq):
        self.R, self.C, self.A, self.B = dp // 2, 2, 2, 2
        self.I = seq // 4
        self.n = dp * seq
        self.G = self.C * self.I
        self.K = self.R * self.A * self.B

    def flat(self, r, c, a, i, b):
        return (((r * 2 + c) * 2 + a) * self.I + i) * 2 + b

    def here(self):
        me = lax.axis_index(AXES)
        self.me = me
        self.b = me % 2
        self.i = (me // 2) % self.I
        self.a = (me // (2 * self.I)) % 2
        self.c = (me // (4 * self.I)) % 2
        self.r = me // (8 * self.I)

    def send(self, array, move):
        pairs = []
        for r in range(self.R):
            for c in range(2):
                for a in range(2):
                    for i in range(self.I):
                        for b in range(2):
                            pairs.append(
                                (self.flat(r, c, a, i, b), self.flat(*move(r, c, a, i, b)))
                            )
        return lax.ppermute(array, AXES, pairs)

    def everyone(self, row):
        return lax.all_to_all(jnp.broadcast_to(row[None], (self.n,) + row.shape), AXES, 0, 0)

    def swap_cores(self, array):
        return self.send(array, lambda r, c, a, i, b: (r, 1 - c, a, i, b))

    def far_chips(self, own):
        return [
            self.send(own, lambda r, c, a, i, b: (r, c, a, (i - di) % self.I, b))
            for di in range(1, self.I)
        ]

    def both_cores(self, array):
        return jnp.concatenate([array, self.swap_cores(array)])

    def join_cores(self, part):
        half = part.shape[0] // 2
        return part[:half] + self.swap_cores(part[half:].astype(BF16)).astype(F32)

    def return_chip(self, joint, di):
        return self.send(
            joint.astype(BF16), lambda r, c, a, i, b: (r, c, a, (i + di) % self.I, b)
        )

    def exchange(self, blocks):
        return lax.all_to_all(blocks, MEMBERS, 0, 0)

    def steps(self, order):
        found = []
        for name in order:
            if name == "a":
                found.append((1, 0, self.a, lambda r, c, a, i, b: (r, c, 1 - a, i, b)))
            elif name == "b":
                found.append((2, 0, self.b, lambda r, c, a, i, b: (r, c, a, i, 1 - b)))
            else:
                for bit in range(int(math.log2(self.R))):
                    found.append(
                        (
                            0,
                            bit,
                            (self.r >> bit) & 1,
                            lambda r, c, a, i, b, bit=bit: (r ^ (1 << bit), c, a, i, b),
                        )
                    )
        return found


class Gathering:
    def __init__(self, grid, piece, order):
        self.grid, self.gathered, self.got = grid, piece[None], None
        self.moves = grid.steps(order)
        self.places = [(0, 0, 0)]

    def land(self, after):
        if self.got is not None:
            self.gathered = jnp.concatenate([self.gathered, tie(self.got, *after)])
            self.got = None

    def step(self, *after):
        self.land(after)
        axis, bit, unused, move = self.moves.pop(0)
        self.got = self.grid.send(tie(self.gathered, *after), move)
        moved = tuple((1 << bit) if axis == j else 0 for j in range(3))
        self.places = self.places + [
            tuple(p ^ q for p, q in zip(place, moved)) for place in self.places
        ]

    def finish(self, *after):
        while self.moves:
            self.step(*after)
        self.land(after)
        grid, found_at = self.grid, []
        for r in range(grid.R):
            for a in range(2):
                for b in range(2):
                    index = 0
                    for k, (pr, pa, pb) in enumerate(self.places):
                        found = ((grid.r ^ pr) == r) & ((grid.a ^ pa) == a) & ((grid.b ^ pb) == b)
                        index = index + jnp.where(found, k, 0)
                    found_at.append(index)
        return self.gathered, jnp.stack(found_at).astype(jnp.int32)


class Scattering:
    def __init__(self, grid, parts, order, axes):
        self.grid, self.parts, self.got = grid, parts, None
        self.moves = [
            (axes[axis], up, move) for axis, bit, up, move in reversed(grid.steps(order))
        ]

    def land(self, after):
        if self.got is not None:
            self.parts = self.keep.astype(F32) + tie(self.got, *after).astype(F32)
            self.got = None

    def step(self, *after):
        self.land(after)
        axis, up, move = self.moves.pop(0)
        half = self.parts.shape[axis] // 2
        self.keep = lax.dynamic_slice_in_dim(self.parts, up * half, half, axis)
        give = lax.dynamic_slice_in_dim(self.parts, (1 - up) * half, half, axis)
        self.got = self.grid.send(give.astype(BF16), move)

    def finish(self, *after):
        while self.moves:
            self.step(*after)
        self.land(after)
        return self.parts


class Order:
    def __init__(self):
        self.last = None

    def use(self, value):
        return value if self.last is None else tie(value, self.last)

    def did(self, value):
        self.last = value
        return value


def normalized(values):
    center = jnp.mean(values, axis=-1, keepdims=True)
    shifted = values - center
    spread = jnp.mean(shifted * shifted, axis=-1, keepdims=True)
    rate = lax.rsqrt(spread + EPSILON)
    return shifted * rate, rate


def layer_norm(values, gain, bias):
    unit, rate = normalized(values)
    return unit * gain + bias


def norm_back(values, gain, gradient):
    unit, rate = normalized(values)
    scaled = gradient * gain
    mean_grad = jnp.mean(scaled, axis=-1, keepdims=True)
    mean_along = jnp.mean(scaled * unit, axis=-1, keepdims=True)
    return (
        rate * (scaled - mean_grad - unit * mean_along),
        jnp.sum(gradient * unit, axis=0),
        jnp.sum(gradient, axis=0),
    )


def gelu_gate(values):
    return 0.5 + 0.5 * lax.erf(values * math.sqrt(0.5))


def gelu_slope(values):
    density = jnp.exp(-0.5 * values * values) * (1.0 / math.sqrt(2.0 * math.pi))
    return gelu_gate(values) + values * density


LANES = 128
SCALE = 1.0 / math.sqrt(HEAD)


def in_head(values, head):
    lane = lax.broadcasted_iota(jnp.int32, values.shape, 1)
    inside = (lane >= head * HEAD) & (lane < (head + 1) * HEAD)
    return jnp.where(inside, values, jnp.zeros_like(values))


def inner(left, right, left_dim, right_dim):
    return lax.dot_general(
        left, right, (((left_dim,), (right_dim,)), ((), ())), preferred_element_type=F32
    )


def allowed(causal, key_docs, query_docs, key_places, query_places):
    mask = key_docs[...] == query_docs[...]
    if causal:
        mask = mask & (key_places[...] <= query_places[...])
    return mask


def head_rows(values, head):
    row = lax.broadcasted_iota(jnp.int32, values.shape, 0)
    inside = (row >= head * HEAD) & (row < (head + 1) * HEAD)
    return jnp.where(inside, values, jnp.zeros_like(values))


def turned(values):
    return jnp.transpose(values.astype(F32)).astype(values.dtype)


def attend_kernel(
    causal, q, k, v, key_docs, query_docs, key_places, query_places, mixed, log_total, v_turned
):
    @pl.when(pl.program_id(1) == 0)
    def turn():
        v_turned[...] = turned(v[...])

    mask = allowed(causal, key_docs, query_docs, key_places, query_places)
    queries = q[...] * jnp.asarray(SCALE, BF16)
    result = None
    for head in range(LANES // HEAD):
        scores = inner(k[...], in_head(queries, head), 1, 1)
        scores = jnp.where(mask, scores, MASK_VALUE)
        row_max = jnp.max(scores, axis=0, keepdims=True)
        exponent = jnp.exp(scores - row_max)
        row_sum = jnp.sum(exponent, axis=0, keepdims=True)
        attention = (exponent * (1.0 / row_sum)).astype(BF16)
        part = head_rows(inner(v_turned[...], attention, 1, 0), head)
        result = part if result is None else result + part
        log_total[0, head : head + 1, :] = row_max + jnp.log(row_sum)
    mixed[...] = jnp.transpose(result).astype(BF16)


def attend_back_kernel(
    causal,
    q,
    k,
    v,
    key_docs,
    query_docs,
    key_places,
    query_places,
    log_total,
    grad_mixed,
    grads,
    grad_keys,
    grad_values,
    k_turned,
):
    pair, tile = pl.program_id(0), pl.program_id(1)
    pairs, tiles = pl.num_programs(0), pl.num_programs(1)
    size = q.shape[0]

    @pl.when(tile == 0)
    def clear():
        grad_keys[...] = jnp.zeros_like(grad_keys)
        grad_values[...] = jnp.zeros_like(grad_values)
        k_turned[...] = turned(k[...])

    mask = allowed(causal, key_docs, query_docs, key_places, query_places)
    queries = q[...] * jnp.asarray(SCALE, BF16)
    grad_queries = None
    for head in range(LANES // HEAD):
        head_queries = in_head(queries, head)
        head_grad = in_head(grad_mixed[...], head)
        scores = jnp.where(mask, inner(k[...], head_queries, 1, 1), MASK_VALUE)
        attention = jnp.exp(scores - log_total[0, head : head + 1, :])
        grad_attention = inner(v[...], head_grad, 1, 1)
        row_delta = jnp.sum(attention * grad_attention, axis=0, keepdims=True)
        grad_scores = (attention * (grad_attention - row_delta)).astype(BF16)
        grad_values[...] += inner(attention.astype(BF16), head_grad, 1, 0)
        grad_keys[...] += inner(grad_scores, head_queries, 1, 0)
        part = head_rows(inner(k_turned[...], grad_scores, 1, 0), head)
        grad_queries = part if grad_queries is None else grad_queries + part

    def column(block):
        return pl.ds(pl.multiple_of(block * LANES, LANES), LANES)

    grads[pl.ds(pl.multiple_of(tile * size, size), size), column(pair)] = jnp.transpose(
        grad_queries * SCALE
    ).astype(BF16)

    @pl.when(tile == tiles - 1)
    def store():
        grads[:, column(pairs + pair)] = grad_keys[...].astype(BF16)
        grads[:, column(2 * pairs + pair)] = grad_values[...].astype(BF16)


def attend_specs(rows, tile, offsets, first):
    def keys(offset):
        return pl.BlockSpec((rows, LANES), lambda p, i: (0, offset + p))

    row = pl.BlockSpec((1, tile), lambda p, i: (0, first + i))
    column = pl.BlockSpec((rows, 1), lambda p, i: (0, 0))
    return [
        pl.BlockSpec((tile, LANES), lambda p, i: (first + i, offsets[0] + p)),
        keys(offsets[1]),
        keys(offsets[2]),
        column,
        row,
        column,
        row,
    ]


VMEM_BYTES = 48 * 1024 * 1024


def attend_call(arrays, offsets, meta, causal, part, start, count):
    rows = arrays[0].shape[0]
    pairs, tile = part // LANES, min(count, 256)
    places = [offset // LANES for offset in offsets]
    return pl.pallas_call(
        functools.partial(attend_kernel, causal),
        grid=(pairs, count // tile),
        in_specs=attend_specs(rows, tile, places, start // tile),
        out_specs=[
            pl.BlockSpec((tile, LANES), lambda p, i: (i, p)),
            pl.BlockSpec((1, LANES // HEAD, tile), lambda p, i: (p, 0, i)),
        ],
        out_shape=[
            jax.ShapeDtypeStruct((count, part), BF16),
            jax.ShapeDtypeStruct((pairs, LANES // HEAD, count), F32),
        ],
        scratch_shapes=[pltpu.VMEM((LANES, rows), BF16)],
        compiler_params=pltpu.CompilerParams(vmem_limit_bytes=VMEM_BYTES),
        cost_estimate=pl.CostEstimate(flops=0, bytes_accessed=0, transcendentals=0),
        name="attend",
    )(*arrays, *meta)


def attend_back_call(arrays, offsets, meta, causal, part, log_total, grad_mixed):
    rows = arrays[0].shape[0]
    pairs, tile = part // LANES, min(rows, 256)
    places = [offset // LANES for offset in offsets]
    return pl.pallas_call(
        functools.partial(attend_back_kernel, causal),
        grid=(pairs, rows // tile),
        in_specs=attend_specs(rows, tile, places, 0)
        + [
            pl.BlockSpec((1, LANES // HEAD, tile), lambda p, i: (p, 0, i)),
            pl.BlockSpec((tile, LANES), lambda p, i: (i, p)),
        ],
        out_specs=pl.BlockSpec((rows, 3 * part), lambda p, i: (0, 0)),
        out_shape=jax.ShapeDtypeStruct((rows, 3 * part), BF16),
        scratch_shapes=[
            pltpu.VMEM((rows, LANES), F32),
            pltpu.VMEM((rows, LANES), F32),
            pltpu.VMEM((LANES, rows), BF16),
        ],
        compiler_params=pltpu.CompilerParams(vmem_limit_bytes=VMEM_BYTES),
        cost_estimate=pl.CostEstimate(flops=0, bytes_accessed=0, transcendentals=0),
        name="attend_back",
    )(*arrays, *meta, log_total, grad_mixed)


def layout_call(kernel, outs, name, tables, arrays):
    whole = pl.BlockSpec(memory_space=pltpu.VMEM)
    return pl.pallas_call(
        kernel,
        grid_spec=pltpu.PrefetchScalarGridSpec(
            num_scalar_prefetch=len(tables),
            grid=(),
            in_specs=[whole] * len(arrays),
            out_specs=[whole] * len(outs),
        ),
        out_shape=outs,
        compiler_params=pltpu.CompilerParams(vmem_limit_bytes=VMEM_BYTES),
        cost_estimate=pl.CostEstimate(flops=0, bytes_accessed=0, transcendentals=0),
        name=name,
    )(*tables, *arrays)


def place(gathered, rows_at, outs, moves):
    def kernel(rows_ref, source, *targets):
        columns = source.shape[2]
        for out, row, column, k, first, count in moves:
            targets[out][row : row + count, column : column + columns] = source[
                rows_ref[k], first : first + count, :
            ]

    shapes = [jax.ShapeDtypeStruct(shape, gathered.dtype) for shape in outs]
    return layout_call(kernel, shapes, "place", [rows_at], [gathered])


def fold(matrix, columns):
    return jnp.concatenate(jnp.split(matrix, matrix.shape[-1] // columns, axis=-1), axis=-2)


def unfold(matrix, rows):
    return jnp.concatenate(jnp.split(matrix, matrix.shape[-2] // rows, axis=-2), axis=-1)


def local(
    dp,
    seq,
    source_embed,
    target_embed,
    source_docs,
    target_docs,
    label_index,
    label_token,
    attend_in,
    attend_out,
    feed_up,
    feed_down,
    norm_gain,
    norm_bias,
    vocab_table,
):
    micro, unused, tokens, width = source_embed.shape
    labels = label_index.shape[2]
    norms, share = norm_gain.shape
    hidden_share = feed_down.shape[1]
    grid = Grid(dp, seq)
    grid.here()
    R, I, G, K, n = grid.R, grid.I, grid.G, grid.K, grid.n
    part = width // G
    hid = hidden_share * K

    def to_row(embed):
        got = []
        for k in range(micro):
            message = jnp.where((grid.b ^ k) == 0, embed[0, 0], embed[1, 0])
            got.append(grid.send(message, lambda r, c, a, i, b: (r, a, b ^ k, i, c)))
        return jnp.where(grid.a == 0, jnp.concatenate(got), jnp.concatenate(got[::-1])).astype(F32)

    def from_row(gradient):
        gradient = gradient.astype(BF16)
        got = []
        for k in range(micro):
            message = jnp.where((grid.a ^ k) == 0, gradient[:tokens], gradient[tokens:])
            got.append(grid.send(message, lambda r, c, a, i, b: (r, b, c, i, a ^ k)))
        return jnp.where(grid.b == 0, jnp.stack(got), jnp.stack(got[::-1])).astype(F32)[:, None]

    kernels = share % 16 == 0 and hidden_share % 16 == 0 and part % LANES == 0

    def member_rows(k, member):
        return grid.flat(k // 4, member // I, k // 2 % 2, member % I, k % 2) * share

    def natural_in(found):
        gathered, rows_at = found
        if not kernels:
            gathered = jnp.take(gathered, rows_at, axis=0).reshape(R, 2, 2, 2, I, 3, share, part)
            return gathered.transpose(0, 3, 1, 4, 2, 6, 5, 7).reshape(width, 3 * part)
        moves = [
            (0, member_rows(k, member), j * part, k, (member * 3 + j) * share, share)
            for k in range(K)
            for member in range(G)
            for j in range(3)
        ]
        return place(gathered, rows_at, [(width, 3 * part)], moves)[0]

    def natural_out(found):
        gathered, rows_at = found
        if not kernels:
            gathered = jnp.take(gathered, rows_at, axis=0)
            return [
                gathered[:, i * share : (i + 1) * share].reshape(part, width) for i in range(3)
            ]
        moves = [(i, k * share, 0, k, i * share, share) for k in range(K) for i in range(3)]
        return place(gathered, rows_at, [(part, width)] * 3, moves)

    def out_home(block):
        member, row = block // K, block % K
        return (row // 4, member // I, row // 2 % 2, member % I, row % 2)

    def in_blocks(weight):
        return weight.reshape(-1, G, part).transpose(1, 0, 2)

    first = grid.exchange(in_blocks(attend_in[0].reshape(3 * share, width)))
    in_0 = Gathering(grid, first.reshape(-1, part), "abr")
    in_0.step()
    source = to_row(source_embed)

    small = jnp.concatenate(
        [
            a.astype(F32).reshape(-1)
            for a in (
                norm_gain,
                norm_bias,
                source_docs,
                target_docs,
                label_index,
                label_token,
            )
        ]
    )
    small = grid.everyone(small)
    edges = [0]
    for length in (norms * share, norms * share, micro * tokens, micro * tokens):
        edges.append(edges[-1] + length)
    for length in (micro * labels, micro * labels):
        edges.append(edges[-1] + length)
    pieces = [small[:, edges[i] : edges[i + 1]] for i in range(6)]
    rows = small[:, : edges[2]].reshape(n, 2 * norms, share).transpose(1, 0, 2)
    rows = lax.optimization_barrier(rows.reshape(2 * norms, width))
    gains, biases = rows[:norms], rows[norms:]

    def row_of(piece, length):
        whole = piece.reshape(R, 2, 2, I, 2, micro, length)
        whole = lax.dynamic_index_in_dim(whole, grid.r, 0, False)
        whole = lax.dynamic_index_in_dim(whole, grid.b, 0, False)
        return lax.dynamic_index_in_dim(whole, grid.a, 3, False)

    def row_order(values):
        values = values.transpose(1, 0, 2, 3)
        values = jnp.where(grid.c == 0, values, values[:, ::-1])
        shifted = values
        for shift in range(1, I):
            shifted = jnp.where(grid.i == shift, jnp.roll(values, -shift, axis=0), shifted)
        return shifted.reshape(-1)

    source_row_docs = row_order(row_of(pieces[2], tokens)).astype(jnp.int32)
    target_row_docs = row_order(row_of(pieces[3], tokens)).astype(jnp.int32)
    places = row_order(jnp.arange(4 * I * tokens, dtype=jnp.int32).reshape(2, I, 2, tokens))
    own_index = lax.dynamic_index_in_dim(row_of(pieces[4], labels), grid.c, 0, False)
    own_index = lax.dynamic_index_in_dim(own_index, grid.i, 0, False).astype(jnp.int32)
    slots = jnp.arange(2)[:, None]
    label_rows = (
        own_index - ((grid.c * I + grid.i) * 2 + slots) * tokens + slots * tokens
    ).reshape(-1)
    own_labels = 2 * labels
    every_token = (
        pieces[5]
        .reshape(R, 2, 2, I, 2, micro, labels)
        .transpose(0, 2, 5, 3, 1, 4, 6)
        .reshape(n, own_labels)
        .astype(jnp.int32)
    )

    later_in, feed_up, target_embed, attend_out, unused = lax.optimization_barrier(
        (attend_in[1:], feed_up, target_embed, attend_out, in_0.gathered)
    )
    out_piece = grid.send(
        attend_out, lambda r, c, a, i, b: out_home(grid.flat(r, c, a, i, b))
    ).reshape(3 * share, width)
    ups = feed_up.reshape(2 * share, R, 2, 2, I, 2, hidden_share)
    ups = grid.exchange(ups.transpose(2, 4, 0, 1, 3, 5, 6).reshape(G, 2 * share, hid))
    later_in = grid.exchange(in_blocks(later_in.reshape(6 * share, width)))
    target = to_row(target_embed)

    def in_bundle(which):
        return later_in[:, (which - 1) * 3 * share : which * 3 * share].reshape(-1, part)

    def feed_bundle(which):
        up = ups[:, which * share : (which + 1) * share].reshape(-1, hid)
        return jnp.concatenate([up, fold(feed_down[which], hid)])

    def feed_weights(found):
        gathered, rows_at = found
        folds = width // hid
        if not kernels:
            gathered = jnp.take(gathered, rows_at, axis=0)
            up = gathered[:, : G * share].reshape(R, 2, 2, 2, I, share, hid)
            down = unfold(gathered[:, G * share :], hidden_share)
            return up.transpose(0, 3, 1, 4, 2, 5, 6).reshape(width, hid), down.reshape(hid, width)
        moves = [
            (0, member_rows(k, member), 0, k, member * share, share)
            for k in range(K)
            for member in range(G)
        ]
        for k in range(K):
            for j in range(folds):
                row = G * share + j * hidden_share
                moves.append((1, k * hidden_share, j * hid, k, row, hidden_share))
        return place(gathered, rows_at, [(width, hid), (hid, width)], moves)

    def meta(query_docs, key_docs):
        return (key_docs[:, None], query_docs[None, :], places[:, None], places[None, :])

    source_meta = meta(source_row_docs, source_row_docs)
    target_meta = meta(target_row_docs, target_row_docs)
    cross_meta = meta(target_row_docs, source_row_docs)
    chip = 4 * tokens
    rows = I * chip

    order = Order()

    def launch(own):
        return own, grid.far_chips(own)

    def apply_near(launched, apply):
        chip_rows = order.use(grid.both_cores(launched[0]))
        return chip_rows, order.did(apply(chip_rows, 0))

    def apply_far(launched, apply):
        chips, results = [], []
        for k, array in enumerate(launched[1]):
            chips.append(order.use(grid.both_cores(order.use(array))))
            results.append(order.did(apply(chips[-1], k + 1)))
        return chips, results

    def apply_all(launched, apply):
        near, near_result = apply_near(launched, apply)
        chips, results = apply_far(launched, apply)
        return [near] + chips, [near_result] + results

    def send_far(parts):
        joints = [order.did(grid.join_cores(array)) for array in parts]
        return [grid.return_chip(joint, k + 1) for k, joint in enumerate(joints)]

    def receive(near_part, sent):
        total = grid.join_cores(near_part)
        for array in sent:
            total = total + order.use(array).astype(F32)
        return total

    def attend_far(arrays, offsets, meta_rows, causal):
        held = order.use(arrays[0])
        arrays = [held if array is arrays[0] else array for array in arrays]
        far = attend_call(arrays, offsets, meta_rows, causal, part, chip, rows - chip)
        order.did(far[0])
        return far

    def attend_near(arrays, offsets, meta_rows, causal):
        held = order.use(arrays[0])
        arrays = [held if array is arrays[0] else array for array in arrays]
        near = attend_call(arrays, offsets, meta_rows, causal, part, 0, chip)
        order.did(near[0])
        return near

    def by_far_chip(array):
        return [array[k * chip : (k + 1) * chip] for k in range(I - 1)]

    def stored(near, far):
        return [near[0]] + by_far_chip(far[0]), jnp.concatenate([near[1], far[1]], axis=2)

    def far_product(array, weight):
        return [product(order.use(p), weight) for p in by_far_chip(array)]

    def projection(weight):
        return lambda array, unused: product(array, weight).astype(BF16)

    def rise(weight):
        def apply(normed, unused):
            up = product(normed, weight)
            return (up * gelu_gate(up)).astype(BF16)

        return apply

    self_offsets = (0, part, 2 * part)
    cross_offsets = (0, 0, part)

    out_all = Gathering(grid, out_piece, "arb")
    feed_0 = Gathering(grid, feed_bundle(0), "abr")
    in_1 = Gathering(grid, in_bundle(1), "arb")
    in_2 = Gathering(grid, in_bundle(2), "abr")
    feed_1 = Gathering(grid, feed_bundle(1), "arb")

    enc_start = layer_norm(source, gains[0], biases[0])
    enc_normed = layer_norm(enc_start, gains[1], biases[1]).astype(BF16)
    in_0.step()
    out_all.step(in_0.gathered)
    in_0.step()
    enc_launched = launch(enc_normed)
    dec_start = layer_norm(target, gains[4], biases[4])
    dec_normed = layer_norm(dec_start, gains[5], biases[5]).astype(BF16)
    feed_0.step(out_all.gathered)
    out_all.step(in_0.gathered)
    in_1.step(in_0.gathered)
    w_in_0 = order.did(natural_in(in_0.finish(dec_normed)))
    enc_in, results = apply_all(enc_launched, projection(w_in_0))
    enc_qkv = jnp.concatenate(results)
    in_1.step(order.last)
    feed_0.step(order.last)
    out_all.step(order.last)
    enc_source = ([enc_qkv] * 3, self_offsets, source_meta, False)
    far = attend_far(*enc_source)
    near = attend_near(*enc_source)
    feed_0.step(order.last)
    in_1.step(order.last)
    dec_launched = launch(dec_normed)
    w_out = natural_out(out_all.finish(order.last))
    enc_mixed, enc_log = stored(near, far)
    sent = send_far(far_product(far[0], w_out[0]))
    in_2.step(order.last)
    near_part = product(order.use(near[0]), w_out[0])
    w_in_1 = order.did(natural_in(in_1.finish(order.last)))
    dec_in, results = apply_all(dec_launched, projection(w_in_1))
    dec_qkv = jnp.concatenate(results)
    enc_middle = order.did(enc_start + receive(near_part, sent))
    ff_normed = layer_norm(enc_middle, gains[2], biases[2]).astype(BF16)
    enc_launched = launch(order.did(ff_normed))
    in_2.step(order.last)
    feed_1.step(order.last)
    dec_source = ([dec_qkv] * 3, self_offsets, target_meta, True)
    far = attend_far(*dec_source)
    sent = send_far(far_product(far[0], w_out[1]))
    near = attend_near(*dec_source)
    dec_mixed, dec_log = stored(near, far)
    near_part = product(near[0], w_out[1])
    up_0, down_0 = feed_weights(feed_0.finish(near_part))
    feed_1.step(near_part)
    in_2.step(near_part)
    dec_self = order.did(dec_start + receive(near_part, sent))
    cross_normed = layer_norm(dec_self, gains[6], biases[6]).astype(BF16)
    ff_chips_0, hidden_0 = apply_all(enc_launched, rise(up_0))
    sent = send_far([product(h, down_0) for h in hidden_0[1:]])
    cross_launched = launch(cross_normed)
    enc_end = enc_middle + receive(product(order.use(hidden_0[0]), down_0), sent)
    encoded = order.did(layer_norm(enc_end, gains[3], biases[3]).astype(BF16))
    encoded_launched = launch(encoded)
    w_in_2 = natural_in(in_2.finish(order.last))
    cross_w_q, cross_w_kv = w_in_2[:, :part], w_in_2[:, part:]
    cross_in, results = apply_all(cross_launched, projection(cross_w_q))
    cross_q = jnp.concatenate(results)
    encoded_in, results = apply_all(encoded_launched, projection(cross_w_kv))
    cross_kv = jnp.concatenate(results)
    cross_source = ([cross_q, cross_kv, cross_kv], cross_offsets, cross_meta, False)
    feed_1.step(order.last)
    far = attend_far(*cross_source)
    sent = send_far(far_product(far[0], w_out[2]))
    near = attend_near(*cross_source)
    cross_mixed, cross_log = stored(near, far)
    dec_cross = dec_self + receive(product(near[0], w_out[2]), sent)
    ff_normed = order.did(layer_norm(dec_cross, gains[7], biases[7]).astype(BF16))
    dec_launched = launch(ff_normed)
    up_1, down_1 = feed_weights(feed_1.finish(order.last))
    ff_chips_1, hidden_1 = apply_all(dec_launched, rise(up_1))
    sent = send_far([product(h, down_1) for h in hidden_1[1:]])
    dec_end = dec_cross + receive(product(order.use(hidden_1[0]), down_1), sent)
    final = order.did(layer_norm(dec_end, gains[8], biases[8]))

    all_rows = grid.everyone(jnp.take(final, label_rows, axis=0).astype(BF16))
    all_rows = all_rows.reshape(n * own_labels, width)
    every_token = every_token.reshape(-1)
    vocab_rows = vocab_table.shape[0]
    vocab_places = grid.me * vocab_rows + jnp.arange(vocab_rows, dtype=jnp.int32)
    logits = by_transpose(all_rows, vocab_table)
    target_hit = every_token[:, None] == vocab_places[None, :]
    row_max = jnp.max(logits, axis=-1)
    stats = jnp.stack(
        [
            row_max,
            jnp.sum(jnp.exp(logits - row_max[:, None]), axis=-1),
            jnp.sum(jnp.where(target_hit, logits, 0.0), axis=-1),
        ]
    )
    every_stats = grid.everyone(stats)
    joint = jnp.max(every_stats[:, 0], axis=0)
    total = jnp.sum(every_stats[:, 1] * jnp.exp(every_stats[:, 0] - joint), axis=0)
    stats = (joint, total, jnp.sum(every_stats[:, 2], axis=0))
    log_total = stats[0] + jnp.log(stats[1])
    mean_loss = jnp.sum(log_total - stats[2]) / (n * own_labels)
    grad_logits = (jnp.exp(logits - log_total[:, None]) - target_hit.astype(F32)).astype(BF16)
    grad_rows = product(grad_logits, vocab_table).reshape(n, own_labels, width)
    table_grad = rows_inner(grad_logits, all_rows)
    grad_rows = lax.all_to_all(grad_rows.astype(BF16), AXES, 0, 0)
    grad_rows = jnp.sum(grad_rows.astype(F32), axis=0)
    grad_final = jnp.zeros(final.shape, F32).at[label_rows].add(grad_rows)

    gain_grads = [None] * norms
    bias_grads = [None] * norms

    def back_norm(values, norm, gradient):
        result, gain_grads[norm], bias_grads[norm] = norm_back(values, gains[norm], gradient)
        return result

    def rows_sum(left, right):
        left, right = (
            order.use(a if not isinstance(a, list) else jnp.concatenate(a)) for a in (left, right)
        )
        return order.did(rows_inner(left, right).astype(BF16))

    def far_back(grads, weight):
        return send_far([by_transpose(order.use(g), weight) for g in grads[1:]])

    def near_back(grads, weight):
        return order.did(by_transpose(order.use(grads[0]), weight))

    def fall(chips, up_weight, down_weight):
        def apply(grad, k):
            up = product(chips[k], up_weight)
            return (by_transpose(grad, down_weight) * gelu_slope(up)).astype(BF16)

        return apply

    def back_projection(weight):
        return lambda grad, unused: by_transpose(grad, weight).astype(BF16)

    def attend_back(source, log_total, grad_mixed):
        arrays, offsets, meta_rows, causal = source
        grad_mixed = order.use(jnp.concatenate(grad_mixed))
        return order.did(
            attend_back_call(arrays, offsets, meta_rows, causal, part, log_total, grad_mixed)
        )

    def by_chip(matrix):
        return [matrix[i * chip : (i + 1) * chip] for i in range(I)]

    def feed_scatter(up_grad, down_grad, name):
        up_grad = up_grad.reshape(R, 2, 2, I, 2, share, hid)
        up_grad = up_grad.transpose(0, 2, 4, 1, 3, 5, 6).reshape(R, 2, 2, G * share, hid)
        down_grad = fold(down_grad.reshape(R, 2, 2, hidden_share, width), hid)
        bundle = jnp.concatenate([up_grad, down_grad], axis=3)
        return Scattering(grid, bundle, name, (0, 1, 2))

    def settle_feed(total):
        total = total[0, 0, 0]
        up = grid.exchange(total[: G * share].reshape(G, share, hid).astype(BF16))
        up = up.reshape(2, I, share, R, 2, 2, hidden_share).transpose(2, 3, 0, 4, 1, 5, 6)
        return up.reshape(share, -1).astype(F32), unfold(total[G * share :], hidden_share)

    def in_scatter(grads, name):
        grads = grads.reshape(R, 2, 2, I, 2, share, 3 * part)
        return Scattering(grid, grads, name, (0, 2, 4))

    def settle_in(total):
        total = grid.exchange(total.reshape(G, share, 3 * part).astype(BF16)).astype(F32)
        return total.reshape(G, share, 3, part).transpose(2, 1, 0, 3).reshape(3, share, width)

    grad_dec_end = back_norm(dec_end, 8, grad_final)
    launched = launch(order.did(grad_dec_end.astype(BF16)))
    branch, grad_ups = apply_all(launched, fall(ff_chips_1, up_1, down_1))
    sent = far_back(grad_ups, up_1)
    near_part = near_back(grad_ups, up_1)
    feed_1 = feed_scatter(
        rows_sum(ff_chips_1, grad_ups), rows_sum(hidden_1, branch), "abr"
    )
    feed_1.step(order.last)
    grad_dec_cross = grad_dec_end + back_norm(dec_cross, 7, receive(near_part, sent))

    launched = launch(order.did(grad_dec_cross.astype(BF16)))
    branch, grad_mixed = apply_all(launched, back_projection(w_out[2]))
    grads = attend_back(cross_source, cross_log, grad_mixed)
    grad_q, grad_kv = grads[:, :part], grads[:, part:]
    sent_kv = far_back(by_chip(grad_kv), cross_w_kv)
    sent_q = far_back(by_chip(grad_q), cross_w_q)
    near_kv = near_back(by_chip(grad_kv), cross_w_kv)
    near_q = near_back(by_chip(grad_q), cross_w_q)
    out_2 = rows_sum(cross_mixed, branch)
    grad_enc_end = back_norm(enc_end, 3, receive(near_kv, sent_kv))
    enc_launched = launch(order.did(grad_enc_end.astype(BF16)))
    in_grad_q = rows_sum(cross_in, grad_q)
    in_grad_kv = rows_sum(encoded_in, grad_kv)
    in_2 = in_scatter(jnp.concatenate([in_grad_q, in_grad_kv], axis=1), "arb")
    in_2.step(order.last)
    grad_dec_self = grad_dec_cross + back_norm(dec_self, 6, receive(near_q, sent_q))
    dec_launched = launch(order.did(grad_dec_self.astype(BF16)))
    feed_1.step(order.last)

    enc_branch, grad_ups = apply_all(enc_launched, fall(ff_chips_0, up_0, down_0))
    sent = far_back(grad_ups, up_0)
    near_part = near_back(grad_ups, up_0)
    feed_0 = feed_scatter(
        rows_sum(ff_chips_0, grad_ups), rows_sum(hidden_0, enc_branch), "abr"
    )
    feed_0.step(order.last)
    in_2.step(order.last)
    grad_enc_middle = grad_enc_end + back_norm(enc_middle, 2, receive(near_part, sent))
    enc_launched = launch(order.did(grad_enc_middle.astype(BF16)))
    feed_1.step(order.last)
    dec_branch, grad_mixed = apply_all(dec_launched, back_projection(w_out[1]))
    grads_1 = attend_back(dec_source, dec_log, grad_mixed)
    in_2.step(order.last)

    branch, grad_mixed = apply_all(enc_launched, back_projection(w_out[0]))
    sent_1 = far_back(by_chip(grads_1), w_in_1)
    grads_0 = attend_back(enc_source, enc_log, grad_mixed)
    sent_0 = far_back(by_chip(grads_0), w_in_0)
    near_0 = near_back(by_chip(grads_0), w_in_0)
    near_1 = near_back(by_chip(grads_1), w_in_1)
    feed_0.step(order.last)
    in_0 = in_scatter(rows_sum(enc_in, grads_0), "arb")
    in_0.step(order.last)
    in_1 = in_scatter(rows_sum(dec_in, grads_1), "abr")
    in_1.step(order.last)
    grad_enc_start = grad_enc_middle + back_norm(enc_start, 1, receive(near_0, sent_0))
    source_grad = from_row(order.did(back_norm(source, 0, grad_enc_start)))
    grad_dec_start = grad_dec_self + back_norm(dec_start, 5, receive(near_1, sent_1))
    target_grad = from_row(order.did(back_norm(target, 4, grad_dec_start)))
    outs = [rows_sum(enc_mixed, branch), rows_sum(dec_mixed, dec_branch), out_2]
    out_grads = jnp.concatenate([g.reshape(R, 2, 2, share, width) for g in outs], axis=3)
    out_all = Scattering(grid, out_grads, "abr", (0, 1, 2))
    out_all.step(order.last)
    feed_0.step(order.last)
    in_0.step(order.last)
    in_1.step(order.last)

    def out_owner(r, c, a, i, b):
        block = (c * I + i) * K + (r * 2 + a) * 2 + b
        return (
            block // (8 * I),
            block // (4 * I) % 2,
            block // (2 * I) % 2,
            block // 2 % I,
            block % 2,
        )

    feed_1 = settle_feed(feed_1.finish())
    in_2 = settle_in(in_2.finish())
    in_1 = settle_in(in_1.finish())
    feed_0 = settle_feed(feed_0.finish())
    attend_out_grad = grid.send(out_all.finish().reshape(3, share, width), out_owner)
    in_0 = settle_in(in_0.finish())

    norm_grads = jnp.stack(gain_grads + bias_grads)
    norm_grads = norm_grads.reshape(2 * norms, n, share).transpose(1, 0, 2)
    norm_grads = jnp.sum(lax.all_to_all(norm_grads, AXES, 0, 0), axis=0)

    return (
        mean_loss,
        source_grad,
        target_grad,
        jnp.stack([in_0, in_1, in_2]),
        attend_out_grad,
        jnp.stack([feed_0[0], feed_1[0]]),
        jnp.stack([feed_0[1], feed_1[1]]),
        norm_grads[:norms],
        norm_grads[norms:],
        table_grad,
    )


def solution(mesh):
    dp, seq = mesh.shape["dp"], mesh.shape["seq"]
    mesh = jax.sharding.Mesh(mesh.devices.reshape(dp // 2, 2, 2, seq // 4, 2), AXES)

    def placed_local(*arrays):
        return local(dp, seq, *arrays)

    rows = P(None, ("r", "c"), ("a", "i", "b"), None)
    flat = P(None, ("r", "c"), ("a", "i", "b"))
    weight = P(None, AXES, None)
    weight_in = P(None, None, AXES, None)
    norm = P(None, AXES)
    table = P(AXES, None)
    return jax.shard_map(
        placed_local,
        mesh=mesh,
        in_specs=(
            (rows, rows, flat, flat, flat, flat)
            + (weight_in, weight, weight, weight, norm, norm, table)
        ),
        out_specs=(P(), rows, rows, weight_in, weight, weight, weight, norm, norm, table),
        check_vma=False,
    )
```

time: 5380 us -> 1020 us (0.19)
  waiting for transfers between devices: 3170 us -> 333 us
  blocking collectives: 936 us -> 41.1 us
  matrix products: 566 us -> 85.3 us
  local copies, waits for them, and re-layouts: 339 us -> 114 us
  starting transfers between devices: 50 us -> 168 us
  other arithmetic: 267 us -> 150 us
  Pallas kernels: 0 us -> 109 us
    reduce_scatter x4 -> x0, waiting for transfers between devices: 2480 us -> none  [the longest x1 796 us: local(): lax.psum_scatter(whole_in, ('dp', 'seq'), scatter_dimension=2, tiled=True)]
    all_gather x25 -> x0, blocking collectives: 858 us -> none  [the longest x6 193 us: attend_backward(): lax.all_gather(row_delta, 'seq', axis=1, tiled=True)]
    all_gather x28 -> x0, waiting for transfers between devices: 445 us -> none  [the longest x6 151 us: attend_forward(): lax.all_gather(own_values, 'seq', axis=0, tiled=True)]
    dot_general x80 -> x23, matrix products: 435 us -> 30.9 us  [product(): return jnp.dot(left, right, preferred_element_type=F32)]
    ppermute x0 -> x112, waiting for transfers between devices: none -> 286 us  [send(): return lax.ppermute(array, AXES, pairs)]
    unnamed x54 -> x0, waiting for transfers between devices: 241 us -> none
    add x165 -> x28, other arithmetic: 184 us -> 33.3 us  [the longest x15 20.5 us: land(): self.parts = self.keep.astype(F32) + tie(self.got, *after).astype(F32)]
    dynamic_slice x154 -> x6, local copies, waits for them, and re-layouts: 126 us -> 4.9 us  [the longest x4 4.88 us: step(): give = lax.dynamic_slice_in_dim(self.parts, (1 - up) * half, half, axis)]
  transfers between devices with their start and end apart: 51 -> 123, of which waited for: 17 -> 42; matrix products, arithmetic and copies ran while one was open for 22% -> 27% of each run, Pallas kernels for 0% -> 9%
where the time goes in v1:
time: 1020 us; the launch traced here: 1010 us
  waiting for transfers between devices  333 us (33%)
  starting transfers between devices  168 us (16%)
  other arithmetic  150 us (15%)
  local copies, waits for them, and re-layouts  114 us (11%)
  Pallas kernels  109 us (11%)
  matrix products  85.3 us (8%)
  blocking collectives  41.1 us (4%)
    ppermute x112, waiting for transfers between devices, send(): return lax.ppermute(array, AXES, pairs)  286 us
    ppermute x112, starting transfers between devices, send(): return lax.ppermute(array, AXES, pairs)  114 us
    pallas_call x3, Pallas kernels, attend_back_call(): pl.pallas_call(functools.partial(attend_back_kernel, causal), grid=(pairs...  51.3 us
    pallas_call x6, Pallas kernels, attend_call(): pl.pallas_call(functools.partial(attend_kernel, causal), grid=(pairs, cou...  49.6 us
    all_to_all x8, starting transfers between devices, exchange(): return lax.all_to_all(blocks, MEMBERS, 0, 0)  39.5 us
    unnamed x576, local copies, waits for them, and re-layouts  34 us
    dot_general x23, matrix products, product(): return jnp.dot(left, right, preferred_element_type=F32)  30.9 us
    all_to_all x1, blocking collectives, local(): grad_rows = lax.all_to_all(grad_rows.astype(BF16), AXES, 0, 0)  28.9 us
  transfers between devices with their start and end apart: 123, of which 42 were waited for; matrix products, arithmetic and copies ran while one was open for 27% of the time, Pallas kernels for 9%

profile of v1, /device:TPU:8, one launch (start us, length us, event | category | flops | bytes accessed | tf_op | source)
XLA Modules:
  0.0 1008.6 jit_solution(17734174391314618339)
XLA Ops:
  22.0 8.5 collective-permute-done.7
  64.0 11.3 %collective-permute-done.3 = bf16[1,384,256]{2,1,0:T(8,128)(2,1)S(1)} collective-permute-done((bf16[1,384,256]{2,1,0:T(8,128)(2,1)S(1)}, bf16[1,384,256]{2,1,0:T(8,128)(2,1)S(1)}, u32[]{:S(2)}, u32[]{:S(2)}) %collective-permute-start.3) | collective-permute-done | bytes 196640 | tf_op jit(solution)/shard_map/ppermute | solution.py:68
  93.3 14.9 %collective-permute-done.10 = bf16[4,384,256]{2,1,0:T(8,128)(2,1)S(1)} collective-permute-done((bf16[4,384,256]{2,1,0:T(8,128)(2,1)S(1)}, bf16[4,384,256]{2,1,0:T(8,128)(2,1)S(1)}, u32[]{:S(2)}, u32[]{:S(2)}) %collective-permute-start.10) | collective-permute-done | bytes 786464 | tf_op jit(solution)/shard_map/ppermute | solution.py:68
  130.8 7.4 collective-permute-done.16
  150.4 8.2 attend.6
  158.6 8.2 attend.7
  177.1 11.5 %collective-permute-done.13 = bf16[4,384,256]{2,1,0:T(8,128)(2,1)S(1)} collective-permute-done((bf16[4,384,256]{2,1,0:T(8,128)(2,1)S(1)}, bf16[4,384,256]{2,1,0:T(8,128)(2,1)S(1)}, u32[]{:S(2)}, u32[]{:S(2)}) %collective-permute-start.13) | collective-permute-done | bytes 786464 | tf_op jit(solution)/shard_map/ppermute | solution.py:68
  193.3 16.7 %collective-permute-done.29 = bf16[2,256,1024]{2,1,0:T(8,128)(2,1)} collective-permute-done((bf16[2,256,1024]{2,1,0:T(8,128)(2,1)}, bf16[2,256,1024]{2,1,0:T(8,128)(2,1)}, u32[]{:S(2)}, u32[]{:S(2)}) %collective-permute-start.29) | collective-permute-done | bytes 1048608 | tf_op jit(solution)/shard_map/ppermute | solution.py:68
  215.6 9.7 collective-permute-done.22
  227.5 8.4 attend.8
  239.6 8.2 attend.9
  283.5 9.9 collective-permute-done.35
  309.6 8.7 collective-permute-done.41
  321.3 8.5 attend.10
  330.6 11.6 %collective-permute-done.48 = bf16[1,256,1024]{2,1,0:T(8,128)(2,1)S(1)} collective-permute-done((bf16[1,256,1024]{2,1,0:T(8,128)(2,1)S(1)}, bf16[1,256,1024]{2,1,0:T(8,128)(2,1)S(1)}, u32[]{:S(2)}, u32[]{:S(2)}) %collective-permute-start.48) | collective-permute-done | bytes 524320 | tf_op jit(solution)/shard_map/ppermute | solution.py:68
  347.7 8.1 attend.11
  356.5 10.6 %collective-permute-done.49 = bf16[2,256,1024]{2,1,0:T(8,128)(2,1)S(1)} collective-permute-done((bf16[2,256,1024]{2,1,0:T(8,128)(2,1)S(1)}, bf16[2,256,1024]{2,1,0:T(8,128)(2,1)S(1)}, u32[]{:S(2)}, u32[]{:S(2)}) %collective-permute-start.49) | collective-permute-done | bytes 1048608 | tf_op jit(solution)/shard_map/ppermute | solution.py:68
  373.0 40.8 %collective-permute-done.50 = bf16[4,256,1024]{2,1,0:T(8,128)(2,1)S(1)} collective-permute-done((bf16[4,256,1024]{2,1,0:T(8,128)(2,1)S(1)}, bf16[4,256,1024]{2,1,0:T(8,128)(2,1)S(1)}, u32[]{:S(2)}, u32[]{:S(2)}) %collective-permute-start.50) | collective-permute-done | bytes 2097184 | tf_op jit(solution)/shard_map/ppermute | solution.py:68
  442.3 9.7 collective-permute-done.55
  462.7 25.5 %all-to-all-done.4 = bf16[32,12,1024]{2,1,0:T(8,128)(2,1)} async-done(((bf16[32,12,1024]{2,1,0:T(8,128)(2,1)}), bf16[32,12,1024]{2,1,0:T(8,128)(2,1)}, u32[]{:S(2)}, u32[]{:S(2)}) %all-to-all-start.4) | async-done | bytes 786464 | tf_op jit(solution)/shard_map/all_to_all | solution.py:71
  493.2 12.2 %all_to_all.69 = f32[32,3,384]{2,1,0:T(4,128)S(1)} all-to-all(f32[32,3,384]{2,1,0:T(4,128)S(1)} %broadcast_in_dim.29), channel_id=1, replica_groups=mesh['r'=2,'c'=2,'a'=2,'i'=2,'b'=2] {'r','c','a','i','b'}, dimensions={0} | all-to-all | bytes 294912 | tf_op jit(solution)/shard_map/all_to_all | solution.py:71
  509.5 28.9 %all_to_all.70 = bf16[32,12,1024]{2,1,0:T(8,128)(2,1)S(1)} all-to-all(bf16[32,12,1024]{2,1,0:T(8,128)(2,1)S(1)} %convert_element_type.667), channel_id=1, replica_groups=mesh['r'=2,'c'=2,'a'=2,'i'=2,'b'=2] {'r','c','a','i','b'}, dimensions={0} | all-to-all | bytes 1572864 | tf_op jit(solution)/shard_map/all_to_all | solution.py:797
  548.6 9.7 collective-permute-done.57
  594.4 10.2 %collective-permute-done.63 = bf16[256,1024]{1,0:T(8,128)(2,1)S(1)} collective-permute-done((bf16[256,1024]{1,0:T(8,128)(2,1)S(1)}, bf16[256,1024]{1,0:T(8,128)(2,1)S(1)}, u32[]{:S(2)}, u32[]{:S(2)}) %collective-permute-start.63) | collective-permute-done | bytes 524320 | tf_op jit(solution)/shard_map/ppermute | solution.py:68
  611.6 17.1 %attend_back.3 = bf16[1024,768]{1,0:T(8,128)(2,1)S(1)} custom-call(bf16[1024,256]{1,0:T(8,128)(2,1)S(1)} %copy-done.12, bf16[1024,512]{1,0:T(8,128)(2,1)S(1)} %copy-done.7, bf16[1024,512]{1,0:T(8,128)(2,1)S(1)} %copy-done.7, s32[1024,1]{1,0:T(8,128)S(1)} %copy.180.key_docs, s32[1,1024]{1,0:T(1,128)S(1)} %bitcast.262, s32[1024,1]{1,0:T(8,128)S(1)} %copy.181.key_places, ...), custom_call_target="tpu_custom_call" | custom-call | tf_op jit(solution)/shard_map/attend_back/pallas_call | solution.py:384
  660.2 7.7 collective-permute-done.68
  749.1 17.6 %attend_back.4 = bf16[1024,768]{1,0:T(8,128)(2,1)S(1)} custom-call(bf16[1024,768]{1,0:T(8,128)(2,1)S(1)} %copy-done.5, bf16[1024,768]{1,0:T(8,128)(2,1)S(1)} %copy-done.5, bf16[1024,768]{1,0:T(8,128)(2,1)S(1)} %copy-done.5, s32[1024,1]{1,0:T(8,128)S(1)} %copy-done.14, s32[1,1024]{1,0:T(1,128)S(1)} %bitcast.263, s32[1024,1]{1,0:T(8,128)S(1)} %copy.181.key_places, ...), custom_call_target="tpu_custom_call" | custom-call | tf_op jit(solution)/shard_map/attend_back/pallas_call | solution.py:384
  790.0 16.6 %attend_back.5 = bf16[1024,768]{1,0:T(8,128)(2,1)S(1)} custom-call(bf16[1024,768]{1,0:T(8,128)(2,1)S(1)} %copy-done.3, bf16[1024,768]{1,0:T(8,128)(2,1)S(1)} %copy-done.3, bf16[1024,768]{1,0:T(8,128)(2,1)S(1)} %copy-done.3, s32[1024,1]{1,0:T(8,128)S(1)} %copy.180.key_docs, s32[1,1024]{1,0:T(1,128)S(1)} %bitcast.267, s32[1024,1]{1,0:T(8,128)S(1)} %copy.181.key_places, ...), custom_call_target="tpu_custom_call" | custom-call | tf_op jit(solution)/shard_map/attend_back/pallas_call | solution.py:384
  878.6 19.6 %all-to-all-done.12 = f32[32,1,576]{2,1,0:T(1,128)S(1)} async-done(((f32[32,1,576]{2,1,0:T(1,128)}), f32[32,1,576]{2,1,0:T(1,128)S(1)}, u32[]{:S(2)}, u32[]{:S(2)}) %all-to-all-start.12) | async-done | bytes 73760 | tf_op jit(solution)/shard_map/all_to_all | solution.py:948
  940.2 13.7 %collective-permute-done.98 = bf16[1,2,1,2,1,32,768]{6,5,4,3,2,1,0:T(8,128)(2,1)S(1)} collective-permute-done((bf16[1,2,1,2,1,32,768]{6,5,4,3,2,1,0:T(8,128)(2,1)S(1)}, bf16[1,2,1,2,1,32,768]{6,5,4,3,2,1,0:T(8,128)(2,1)S(1)}, u32[]{:S(2)}, u32[]{:S(2)}) %collective-permute-start.98) | collective-permute-done | bytes 196640 | tf_op jit(solution)/shard_map/ppermute | solution.py:68
  954.6 7.2 all-to-all-start.8
  990.9 15.6 %collective-permute-done.105 = f32[3,32,1024]{2,1,0:T(8,128)S(1)} collective-permute-done((f32[3,32,1024]{2,1,0:T(8,128)}, f32[3,32,1024]{2,1,0:T(8,128)S(1)}, u32[]{:S(2)}, u32[]{:S(2)}) %collective-permute-start.105) | collective-permute-done | bytes 393248 | tf_op jit(solution)/shard_map/ppermute | solution.py:68
  (1232 shorter events, 579.1 us)
Async XLA Ops:
  45.7 65.3 %collective-permute-start.8 = (bf16[256,1024]{1,0:T(8,128)(2,1)}, bf16[256,1024]{1,0:T(8,128)(2,1)}, u32[]{:S(2)}, u32[]{:S(2)}) collective-permute-start(bf16[256,1024]{1,0:T(8,128)(2,1)} %add_convert_fusion.4), channel_id=1, source_target_pairs={{0,2},{1,3},{2,0},{3,1},{4,6},{5,7},{6,4},{7,5},{8,10},{9,11},{10,... | collective-permute-start | bytes 1572872 | tf_op jit(solution)/shard_map/ppermute | solution.py:68
  45.7 46.4 %collective-permute-start.9 = (bf16[256,1024]{1,0:T(8,128)(2,1)}, bf16[256,1024]{1,0:T(8,128)(2,1)}, u32[]{:S(2)}, u32[]{:S(2)}) collective-permute-start(bf16[256,1024]{1,0:T(8,128)(2,1)} %add_convert_fusion.4), channel_id=1, source_target_pairs={{0,8},{1,9},{2,10},{3,11},{4,12},{5,13},{6,14},{7,15},{8,0},{9,1},... | collective-permute-start | bytes 1572872 | tf_op jit(solution)/shard_map/ppermute | solution.py:68
  50.4 26.8 %collective-permute-start = (bf16[128,1024]{1,0:T(8,128)(2,1)}, bf16[128,1024]{1,0:T(8,128)(2,1)S(1)}, u32[]{:S(2)}, u32[]{:S(2)}) collective-permute-start(bf16[128,1024]{1,0:T(8,128)(2,1)} %get-tuple-element.415), channel_id=1, source_target_pairs={{0,0},{1,4},{2,2},{3,6},{4,8},{5,12},{6,10},{7,14},{8,1},{9,5},{10... | collective-permute-start | bytes 786440 | tf_op jit(solution)/shard_map/ppermute | solution.py:68
  59.2 59.4 %all-to-all-start.2 = ((bf16[4,192,256]{2,1,0:T(8,128)(2,1)}), bf16[4,192,256]{2,1,0:T(8,128)(2,1)}, u32[]{:S(2)}, u32[]{:S(2)}) async-start(bf16[4,192,256]{2,1,0:T(8,128)(2,1)} %bitcast.296), calls=%async_computation.2 | async-start | bytes 786432 | tf_op jit(solution)/shard_map/all_to_all | solution.py:95
  75.2 39.6 %collective-permute-start.14 = (bf16[3,32,1024]{2,1,0:T(8,128)(2,1)}, bf16[3,32,1024]{2,1,0:T(8,128)(2,1)}, u32[]{:S(2)}, u32[]{:S(2)}) collective-permute-start(bf16[3,32,1024]{2,1,0:T(8,128)(2,1)} %param.20), channel_id=1, source_target_pairs={{0,0},{1,1},{2,4},{3,5},{4,16},{5,17},{6,20},{7,21},{8,2},{9,3},{1... | collective-permute-start | bytes 589832 | tf_op jit(solution)/shard_map/ppermute | solution.py:68
  140.2 28.5 %collective-permute-start.17 = (bf16[4,96,1024]{2,1,0:T(8,128)(2,1)}, bf16[4,96,1024]{2,1,0:T(8,128)(2,1)}, u32[]{:S(2)}, u32[]{:S(2)}) collective-permute-start(bf16[4,96,1024]{2,1,0:T(8,128)(2,1)} %pad_maximum_fusion.55), channel_id=1, source_target_pairs={{0,1},{1,0},{2,3},{3,2},{4,5},{5,4},{6,7},{7,6},{8,9},{9,8},{10,11... | collective-permute-start | bytes 2359304 | tf_op jit(solution)/shard_map/ppermute | solution.py:68
  140.6 34.2 %collective-permute-start.2 = (bf16[256,1024]{1,0:T(8,128)(2,1)}, bf16[256,1024]{1,0:T(8,128)(2,1)}, u32[]{:S(2)}, u32[]{:S(2)}) collective-permute-start(bf16[256,1024]{1,0:T(8,128)(2,1)} %add_convert_fusion.5), channel_id=1, source_target_pairs={{0,8},{1,9},{2,10},{3,11},{4,12},{5,13},{6,14},{7,15},{8,0},{9,1},... | collective-permute-start | bytes 1572872 | tf_op jit(solution)/shard_map/ppermute | solution.py:68
  173.9 36.2 %collective-permute-start.29 = (bf16[2,256,1024]{2,1,0:T(8,128)(2,1)}, bf16[2,256,1024]{2,1,0:T(8,128)(2,1)}, u32[]{:S(2)}, u32[]{:S(2)}) collective-permute-start(bf16[2,256,1024]{2,1,0:T(8,128)(2,1)} %pad_maximum_fusion.33), channel_id=1, source_target_pairs={{0,1},{1,0},{2,3},{3,2},{4,5},{5,4},{6,7},{7,6},{8,9},{9,8},{10,11... | collective-permute-start | bytes 3145736 | tf_op jit(solution)/shard_map/ppermute | solution.py:68
  211.8 46.8 %collective-permute-start.30 = (bf16[4,256,1024]{2,1,0:T(8,128)(2,1)S(1)}, bf16[4,256,1024]{2,1,0:T(8,128)(2,1)}, u32[]{:S(2)}, u32[]{:S(2)}) collective-permute-start(bf16[4,256,1024]{2,1,0:T(8,128)(2,1)S(1)} %pad_maximum_fusion.2), channel_id=1, source_target_pairs={{0,16},{1,17},{2,18},{3,19},{4,20},{5,21},{6,22},{7,23},{8,24},{9,... | collective-permute-start | bytes 6291464 | tf_op jit(solution)/shard_map/ppermute | solution.py:68
  367.3 46.4 %collective-permute-start.50 = (bf16[4,256,1024]{2,1,0:T(8,128)(2,1)S(1)}, bf16[4,256,1024]{2,1,0:T(8,128)(2,1)S(1)}, u32[]{:S(2)}, u32[]{:S(2)}) collective-permute-start(bf16[4,256,1024]{2,1,0:T(8,128)(2,1)S(1)} %pad_maximum_fusion.3), channel_id=1, source_target_pairs={{0,1},{1,0},{2,3},{3,2},{4,5},{5,4},{6,7},{7,6},{8,9},{9,8},{10,11... | collective-permute-start | bytes 6291464 | tf_op jit(solution)/shard_map/ppermute | solution.py:68
  369.7 52.4 %collective-permute-start.51 = (bf16[256,1024]{1,0:T(8,128)(2,1)S(1)}, bf16[256,1024]{1,0:T(8,128)(2,1)}, u32[]{:S(2)}, u32[]{:S(2)}) collective-permute-start(bf16[256,1024]{1,0:T(8,128)(2,1)S(1)} %add_convert_fusion), channel_id=1, source_target_pairs={{0,2},{1,3},{2,0},{3,1},{4,6},{5,7},{6,4},{7,5},{8,10},{9,11},{10,... | collective-permute-start | bytes 1572872 | tf_op jit(solution)/shard_map/ppermute | solution.py:68
  457.3 31.0 %all-to-all-start.4 = ((bf16[32,12,1024]{2,1,0:T(8,128)(2,1)}), bf16[32,12,1024]{2,1,0:T(8,128)(2,1)}, u32[]{:S(2)}, u32[]{:S(2)}) async-start(bf16[32,12,1024]{2,1,0:T(8,128)(2,1)} %broadcast_in_dim.27), calls=%async_computation.4 | async-start | bytes 2097152 | tf_op jit(solution)/shard_map/all_to_all | solution.py:71
  648.5 48.9 %collective-permute-start.109 = (bf16[1,2,2,256,1024]{4,3,2,1,0:T(8,128)(2,1)}, bf16[1,2,2,256,1024]{4,3,2,1,0:T(8,128)(2,1)}, u32[]{:S(2)}, u32[]{:S(2)}) collective-permute-start(bf16[1,2,2,256,1024]{4,3,2,1,0:T(8,128)(2,1)} %fusion.24), channel_id=1, source_target_pairs={{0,16},{1,17},{2,18},{3,19},{4,20},{5,21},{6,22},{7,23},{8,24},{9,... | collective-permute-start | bytes 6291464 | tf_op jit(solution)/shard_map/ppermute | solution.py:68
  681.3 56.9 %collective-permute-start.79 = (bf16[256,1024]{1,0:T(8,128)(2,1)}, bf16[256,1024]{1,0:T(8,128)(2,1)}, u32[]{:S(2)}, u32[]{:S(2)}) collective-permute-start(bf16[256,1024]{1,0:T(8,128)(2,1)} %get-tuple-element.367), channel_id=1, source_target_pairs={{0,2},{1,3},{2,0},{3,1},{4,6},{5,7},{6,4},{7,5},{8,10},{9,11},{10,... | collective-permute-start | bytes 1572872 | tf_op jit(solution)/shard_map/ppermute | solution.py:68
  683.1 30.8 %collective-permute-start.78 = (bf16[256,1024]{1,0:T(8,128)(2,1)}, bf16[256,1024]{1,0:T(8,128)(2,1)}, u32[]{:S(2)}, u32[]{:S(2)}) collective-permute-start(bf16[256,1024]{1,0:T(8,128)(2,1)} %get-tuple-element.367), channel_id=1, source_target_pairs={{0,8},{1,9},{2,10},{3,11},{4,12},{5,13},{6,14},{7,15},{8,0},{9,1},... | collective-permute-start | bytes 1572872 | tf_op jit(solution)/shard_map/ppermute | solution.py:68
  696.7 32.1 %collective-permute-start.99 = (bf16[2,2,2,2,1,32,768]{6,5,4,3,2,1,0:T(8,128)(2,1)}, bf16[2,2,2,2,1,32,768]{6,5,4,3,2,1,0:T(8,128)(2,1)}, u32[]{:S(2)}, u32[]{:S(2)}) collective-permute-start(bf16[2,2,2,2,1,32,768]{6,5,4,3,2,1,0:T(8,128)(2,1)} %constant_dynamic-slice_fusion.1), channel_id=1, source_target_pairs={{0,1},{1,0},{2,3},{3,2},{4,5},{5,4},{6,7},{7,6},{8,9},{9,8},{10,11... | collective-permute-start | bytes 2359304 | tf_op jit(solution)/shard_map/ppermute | solution.py:68
  709.9 32.8 %collective-permute-start.110 = (bf16[1,2,1,256,1024]{4,3,2,1,0:T(8,128)(2,1)}, bf16[1,2,1,256,1024]{4,3,2,1,0:T(8,128)(2,1)}, u32[]{:S(2)}, u32[]{:S(2)}) collective-permute-start(bf16[1,2,1,256,1024]{4,3,2,1,0:T(8,128)(2,1)} %dynamic-slice_convert_fusion), channel_id=1, source_target_pairs={{0,1},{1,0},{2,3},{3,2},{4,5},{5,4},{6,7},{7,6},{8,9},{9,8},{10,11... | collective-permute-start | bytes 3145736 | tf_op jit(solution)/shard_map/ppermute | solution.py:68
  731.6 38.4 %collective-permute-start.100 = (bf16[1,2,2,2,1,32,768]{6,5,4,3,2,1,0:T(8,128)(2,1)}, bf16[1,2,2,2,1,32,768]{6,5,4,3,2,1,0:T(8,128)(2,1)}, u32[]{:S(2)}, u32[]{:S(2)}) collective-permute-start(bf16[1,2,2,2,1,32,768]{6,5,4,3,2,1,0:T(8,128)(2,1)} %dynamic-slice_convert_fusion.5), channel_id=1, source_target_pairs={{0,16},{1,17},{2,18},{3,19},{4,20},{5,21},{6,22},{7,23},{8,24},{9,... | collective-permute-start | bytes 1179656 | tf_op jit(solution)/shard_map/ppermute | solution.py:68
  740.0 97.7 %collective-permute-start.106 = (bf16[1,2,2,256,1024]{4,3,2,1,0:T(8,128)(2,1)}, bf16[1,2,2,256,1024]{4,3,2,1,0:T(8,128)(2,1)}, u32[]{:S(2)}, u32[]{:S(2)}) collective-permute-start(bf16[1,2,2,256,1024]{4,3,2,1,0:T(8,128)(2,1)} %fusion.26), channel_id=1, source_target_pairs={{0,16},{1,17},{2,18},{3,19},{4,20},{5,21},{6,22},{7,23},{8,24},{9,... | collective-permute-start | bytes 6291464 | tf_op jit(solution)/shard_map/ppermute | solution.py:68
  740.9 28.9 %collective-permute-start.81 = (bf16[256,1024]{1,0:T(8,128)(2,1)}, bf16[256,1024]{1,0:T(8,128)(2,1)}, u32[]{:S(2)}, u32[]{:S(2)}) collective-permute-start(bf16[256,1024]{1,0:T(8,128)(2,1)} %get-tuple-element.364), channel_id=1, source_target_pairs={{0,2},{1,3},{2,0},{3,1},{4,6},{5,7},{6,4},{7,5},{8,10},{9,11},{10,... | collective-permute-start | bytes 1572872 | tf_op jit(solution)/shard_map/ppermute | solution.py:68
  746.6 27.0 %collective-permute-start.111 = (bf16[1,1,1,256,1024]{4,3,2,1,0:T(8,128)(2,1)S(1)}, bf16[1,1,1,256,1024]{4,3,2,1,0:T(8,128)(2,1)S(1)}, u32[]{:S(2)}, u32[]{:S(2)}) collective-permute-start(bf16[1,1,1,256,1024]{4,3,2,1,0:T(8,128)(2,1)S(1)} %dynamic-slice_convert_fusion.2), channel_id=1, source_target_pairs={{0,4},{1,5},{2,6},{3,7},{4,0},{5,1},{6,2},{7,3},{8,12},{9,13},{10,... | collective-permute-start | bytes 1572872 | tf_op jit(solution)/shard_map/ppermute | solution.py:68
  780.3 31.4 %all-to-all-start.11 = ((bf16[4,32,1024]{2,1,0:T(8,128)(2,1)}), bf16[4,32,1024]{2,1,0:T(8,128)(2,1)}, u32[]{:S(2)}, u32[]{:S(2)}) async-start(bf16[4,32,1024]{2,1,0:T(8,128)(2,1)} %bitcast.96), calls=%async_computation.11 | async-start | bytes 524288 | tf_op jit(solution)/shard_map/all_to_all | solution.py:95
  824.3 30.6 %collective-permute-start.90 = (bf16[256,1024]{1,0:T(8,128)(2,1)S(1)}, bf16[256,1024]{1,0:T(8,128)(2,1)S(1)}, u32[]{:S(2)}, u32[]{:S(2)}) collective-permute-start(bf16[256,1024]{1,0:T(8,128)(2,1)S(1)} %copy-done.207), channel_id=1, source_target_pairs={{0,2},{1,3},{2,0},{3,1},{4,6},{5,7},{6,4},{7,5},{8,10},{9,11},{10,... | collective-permute-start | bytes 1572872 | tf_op jit(solution)/shard_map/ppermute | solution.py:68
  837.7 62.6 %collective-permute-start.96 = (bf16[1,2,2,2,2,32,768]{6,5,4,3,2,1,0:T(8,128)(2,1)}, bf16[1,2,2,2,2,32,768]{6,5,4,3,2,1,0:T(8,128)(2,1)}, u32[]{:S(2)}, u32[]{:S(2)}) collective-permute-start(bf16[1,2,2,2,2,32,768]{6,5,4,3,2,1,0:T(8,128)(2,1)} %constant_dynamic-slice_fusion.2), channel_id=1, source_target_pairs={{0,16},{1,17},{2,18},{3,19},{4,20},{5,21},{6,22},{7,23},{8,24},{9,... | collective-permute-start | bytes 2359304 | tf_op jit(solution)/shard_map/ppermute | solution.py:68
  849.6 51.4 %collective-permute-start.93 = (bf16[2,2,2,2,1,32,768]{6,5,4,3,2,1,0:T(8,128)(2,1)}, bf16[2,2,2,2,1,32,768]{6,5,4,3,2,1,0:T(8,128)(2,1)}, u32[]{:S(2)}, u32[]{:S(2)}) collective-permute-start(bf16[2,2,2,2,1,32,768]{6,5,4,3,2,1,0:T(8,128)(2,1)} %constant_dynamic-slice_fusion.3), channel_id=1, source_target_pairs={{0,1},{1,0},{2,3},{3,2},{4,5},{5,4},{6,7},{7,6},{8,9},{9,8},{10,11... | collective-permute-start | bytes 2359304 | tf_op jit(solution)/shard_map/ppermute | solution.py:68
  850.3 63.8 %collective-permute-start.107 = (bf16[1,2,1,256,1024]{4,3,2,1,0:T(8,128)(2,1)}, bf16[1,2,1,256,1024]{4,3,2,1,0:T(8,128)(2,1)}, u32[]{:S(2)}, u32[]{:S(2)}) collective-permute-start(bf16[1,2,1,256,1024]{4,3,2,1,0:T(8,128)(2,1)} %dynamic-slice_convert_fusion.1), channel_id=1, source_target_pairs={{0,1},{1,0},{2,3},{3,2},{4,5},{5,4},{6,7},{7,6},{8,9},{9,8},{10,11... | collective-permute-start | bytes 3145736 | tf_op jit(solution)/shard_map/ppermute | solution.py:68
  854.9 50.0 %collective-permute-start.88 = (bf16[128,1024]{1,0:T(8,128)(2,1)}, bf16[128,1024]{1,0:T(8,128)(2,1)}, u32[]{:S(2)}, u32[]{:S(2)}) collective-permute-start(bf16[128,1024]{1,0:T(8,128)(2,1)} %get-tuple-element.407), channel_id=1, source_target_pairs={{0,1},{1,9},{2,3},{3,11},{4,0},{5,8},{6,2},{7,10},{8,5},{9,13},{10... | collective-permute-start | bytes 786440 | tf_op jit(solution)/shard_map/ppermute | solution.py:68
  855.6 50.4 %collective-permute-start.87 = (bf16[128,1024]{1,0:T(8,128)(2,1)}, bf16[128,1024]{1,0:T(8,128)(2,1)}, u32[]{:S(2)}, u32[]{:S(2)}) collective-permute-start(bf16[128,1024]{1,0:T(8,128)(2,1)} %get-tuple-element.406), channel_id=1, source_target_pairs={{0,0},{1,8},{2,2},{3,10},{4,1},{5,9},{6,3},{7,11},{8,4},{9,12},{10... | collective-permute-start | bytes 786440 | tf_op jit(solution)/shard_map/ppermute | solution.py:68
  905.0 32.9 %collective-permute-start.102 = (bf16[1,2,2,96,1024]{4,3,2,1,0:T(8,128)(2,1)}, bf16[1,2,2,96,1024]{4,3,2,1,0:T(8,128)(2,1)S(1)}, u32[]{:S(2)}, u32[]{:S(2)}) collective-permute-start(bf16[1,2,2,96,1024]{4,3,2,1,0:T(8,128)(2,1)} %constant_dynamic-slice_fusion), channel_id=1, source_target_pairs={{0,16},{1,17},{2,18},{3,19},{4,20},{5,21},{6,22},{7,23},{8,24},{9,... | collective-permute-start | bytes 2359304 | tf_op jit(solution)/shard_map/ppermute | solution.py:68
  916.6 46.8 %collective-permute-start.108 = (bf16[1,1,1,256,1024]{4,3,2,1,0:T(8,128)(2,1)}, bf16[1,1,1,256,1024]{4,3,2,1,0:T(8,128)(2,1)}, u32[]{:S(2)}, u32[]{:S(2)}) collective-permute-start(bf16[1,1,1,256,1024]{4,3,2,1,0:T(8,128)(2,1)} %dynamic-slice_convert_fusion.3), channel_id=1, source_target_pairs={{0,4},{1,5},{2,6},{3,7},{4,0},{5,1},{6,2},{7,3},{8,12},{9,13},{10,... | collective-permute-start | bytes 1572872 | tf_op jit(solution)/shard_map/ppermute | solution.py:68
  920.5 33.4 %collective-permute-start.98 = (bf16[1,2,1,2,1,32,768]{6,5,4,3,2,1,0:T(8,128)(2,1)S(1)}, bf16[1,2,1,2,1,32,768]{6,5,4,3,2,1,0:T(8,128)(2,1)S(1)}, u32[]{:S(2)}, u32[]{:S(2)}) collective-permute-start(bf16[1,2,1,2,1,32,768]{6,5,4,3,2,1,0:T(8,128)(2,1)S(1)} %dynamic-slice_convert_fusion.10), channel_id=1, source_target_pairs={{0,4},{1,5},{2,6},{3,7},{4,0},{5,1},{6,2},{7,3},{8,12},{9,13},{10,... | collective-permute-start | bytes 589832 | tf_op jit(solution)/shard_map/ppermute | solution.py:68
  931.5 30.3 %collective-permute-start.95 = (bf16[1,2,1,2,1,32,768]{6,5,4,3,2,1,0:T(8,128)(2,1)S(1)}, bf16[1,2,1,2,1,32,768]{6,5,4,3,2,1,0:T(8,128)(2,1)}, u32[]{:S(2)}, u32[]{:S(2)}) collective-permute-start(bf16[1,2,1,2,1,32,768]{6,5,4,3,2,1,0:T(8,128)(2,1)S(1)} %dynamic-slice_convert_fusion.11), channel_id=1, source_target_pairs={{0,4},{1,5},{2,6},{3,7},{4,0},{5,1},{6,2},{7,3},{8,12},{9,13},{10,... | collective-permute-start | bytes 589832 | tf_op jit(solution)/shard_map/ppermute | solution.py:68
  (380 other events, 5337.1 us)

commit v2 on v1

--- a/solution.py
+++ b/solution.py
@@ -15,6 +15,7 @@
 MASK_VALUE = -1000000000.0
 AXES = ("r", "c", "a", "i", "b")
 MEMBERS = ("c", "i")
+ACROSS = ("r", "a", "b")
 BF16 = jnp.bfloat16
 F32 = jnp.float32
 
@@ -33,6 +34,27 @@
 
 def tie(value, *others):
     return lax.optimization_barrier((value,) + others)[0]
+
+
+def gate_kernel(*refs):
+    pass
+
+
+def gate(value, *others):
+    anywhere = pl.BlockSpec(memory_space=pl.ANY)
+    return pl.pallas_call(
+        gate_kernel,
+        in_specs=[anywhere] * (1 + len(others)),
+        out_specs=anywhere,
+        out_shape=jax.ShapeDtypeStruct(value.shape, value.dtype),
+        input_output_aliases={0: 0},
+        cost_estimate=pl.CostEstimate(flops=int(6e10), bytes_accessed=0, transcendentals=0),
+        name="gate",
+    )(value, *others)
+
+
+def without(kernel, first, count):
+    return lambda *refs: kernel(*refs[:first], *refs[first + count :])
 
 
 class Grid:
@@ -69,6 +91,45 @@
 
     def everyone(self, row):
         return lax.all_to_all(jnp.broadcast_to(row[None], (self.n,) + row.shape), AXES, 0, 0)
+
+    def phases(self):
+        size = self.I
+        core = 4 * size
+        others = [1 << k for k in range(int(math.log2(self.n))) if 1 << k != core]
+        near = [bit for bit in others if bit < 2 * size]
+        groups, rest = [], [bit for bit in others if bit not in near]
+        while rest:
+            groups.append(rest[:2])
+            rest = rest[2:]
+        return groups + [near[k : k + 2] for k in range(0, len(near), 2)] + [[core]]
+
+    def flips(self, group):
+        found = [0]
+        for bit in group:
+            found = found + [bit ^ other for other in found]
+        return found[1:]
+
+    def flip(self, array, mask):
+        return lax.ppermute(array, AXES, [(d, d ^ mask) for d in range(self.n)])
+
+    def spread(self, rows):
+        rows, holders = rows[None], [0]
+        for group in self.phases():
+            masks = self.flips(group)
+            rows = jnp.concatenate([rows] + [self.flip(rows, mask) for mask in masks])
+            holders = holders + [holder ^ mask for mask in masks for holder in holders]
+        return rows, holders
+
+    def collect(self, parts):
+        for group in reversed(self.phases()):
+            masks = self.flips(group)
+            count = parts.shape[0] // (len(masks) + 1)
+            total = parts[:count]
+            for k, mask in enumerate(masks):
+                piece = parts[(k + 1) * count : (k + 2) * count].astype(BF16)
+                total = total + self.flip(piece, mask).astype(F32)
+            parts = total
+        return parts[0]
 
     def swap_cores(self, array):
         return self.send(array, lambda r, c, a, i, b: (r, 1 - c, a, i, b))
@@ -122,17 +183,18 @@
 
     def land(self, after):
         if self.got is not None:
-            self.gathered = jnp.concatenate([self.gathered, tie(self.got, *after)])
+            self.gathered = jnp.concatenate([self.gathered, self.got])
             self.got = None
 
     def step(self, *after):
         self.land(after)
         axis, bit, unused, move = self.moves.pop(0)
-        self.got = self.grid.send(tie(self.gathered, *after), move)
+        self.got = self.grid.send(self.gathered, move)
         moved = tuple((1 << bit) if axis == j else 0 for j in range(3))
         self.places = self.places + [
             tuple(p ^ q for p, q in zip(place, moved)) for place in self.places
         ]
+        return self.gathered
 
     def finish(self, *after):
         while self.moves:
@@ -159,7 +221,7 @@
 
     def land(self, after):
         if self.got is not None:
-            self.parts = self.keep.astype(F32) + tie(self.got, *after).astype(F32)
+            self.parts = self.keep.astype(F32) + self.got.astype(F32)
             self.got = None
 
     def step(self, *after):
@@ -167,8 +229,9 @@
         axis, up, move = self.moves.pop(0)
         half = self.parts.shape[axis] // 2
         self.keep = lax.dynamic_slice_in_dim(self.parts, up * half, half, axis)
-        give = lax.dynamic_slice_in_dim(self.parts, (1 - up) * half, half, axis)
-        self.got = self.grid.send(give.astype(BF16), move)
+        give = lax.dynamic_slice_in_dim(self.parts, (1 - up) * half, half, axis).astype(BF16)
+        self.got = self.grid.send(give, move)
+        return give
 
     def finish(self, *after):
         while self.moves:
@@ -180,12 +243,14 @@
 class Order:
     def __init__(self):
         self.last = None
+        self.kept = False
 
     def use(self, value):
         return value if self.last is None else tie(value, self.last)
 
     def did(self, value):
-        self.last = value
+        if self.kept:
+            self.last = value
         return value
 
 
@@ -224,6 +289,7 @@
 
 
 LANES = 128
+DOCUMENTS = 3
 SCALE = 1.0 / math.sqrt(HEAD)
 
 
@@ -239,13 +305,6 @@
     )
 
 
-def allowed(causal, key_docs, query_docs, key_places, query_places):
-    mask = key_docs[...] == query_docs[...]
-    if causal:
-        mask = mask & (key_places[...] <= query_places[...])
-    return mask
-
-
 def head_rows(values, head):
     row = lax.broadcasted_iota(jnp.int32, values.shape, 0)
     inside = (row >= head * HEAD) & (row < (head + 1) * HEAD)
@@ -256,27 +315,77 @@
     return jnp.transpose(values.astype(F32)).astype(values.dtype)
 
 
+def doc_lanes(docs, head):
+    spare = HEAD if head == 0 else 0
+    lane = lax.broadcasted_iota(jnp.int32, (docs.shape[0], LANES), 1)
+    return lane - spare == docs, (lane >= spare) & (lane < spare + DOCUMENTS)
+
+
+def marked_keys(keys, docs, head):
+    own, any_doc = doc_lanes(docs, head)
+    marks = jnp.where(any_doc & jnp.logical_not(own), MASK_VALUE, 0.0).astype(BF16)
+    return in_head(keys, head) + marks
+
+
+def marked_queries(queries, docs, head):
+    own, unused = doc_lanes(docs, head)
+    return in_head(queries, head) + jnp.where(own, 1.0, 0.0).astype(BF16)
+
+
+def blocked(rows):
+    size = min(rows, 1024)
+    return [slice(start, start + size) for start in range(0, rows, size)]
+
+
 def attend_kernel(
-    causal, q, k, v, key_docs, query_docs, key_places, query_places, mixed, log_total, v_turned
+    causal,
+    q,
+    k,
+    v,
+    key_docs,
+    query_docs,
+    key_places,
+    query_places,
+    mixed,
+    exact,
+    log_total,
+    v_turned,
+    marked,
 ):
+    heads = LANES // HEAD
+
     @pl.when(pl.program_id(1) == 0)
-    def turn():
+    def prepare():
         v_turned[...] = turned(v[...])
-
-    mask = allowed(causal, key_docs, query_docs, key_places, query_places)
+        for head in range(heads):
+            marked[head] = marked_keys(k[...], key_docs[...], head)
+
     queries = q[...] * jnp.asarray(SCALE, BF16)
     result = None
-    for head in range(LANES // HEAD):
-        scores = inner(k[...], in_head(queries, head), 1, 1)
-        scores = jnp.where(mask, scores, MASK_VALUE)
-        row_max = jnp.max(scores, axis=0, keepdims=True)
-        exponent = jnp.exp(scores - row_max)
-        row_sum = jnp.sum(exponent, axis=0, keepdims=True)
-        attention = (exponent * (1.0 / row_sum)).astype(BF16)
-        part = head_rows(inner(v_turned[...], attention, 1, 0), head)
+    for head in range(heads):
+        head_queries = marked_queries(queries, query_docs[...], head)
+        row_max, row_sum, total = None, None, None
+        for rows in blocked(k.shape[0]):
+            scores = inner(marked[head, rows, :], head_queries, 1, 1)
+            if causal:
+                scores = jnp.where(key_places[rows, :] <= query_places[...], scores, MASK_VALUE)
+            block_max = jnp.max(scores, axis=0, keepdims=True)
+            new_max = block_max if row_max is None else jnp.maximum(row_max, block_max)
+            exponent = jnp.exp(scores - new_max)
+            block_sum = jnp.sum(exponent, axis=0, keepdims=True)
+            block = inner(v_turned[:, rows], exponent.astype(BF16), 1, 0)
+            if row_max is None:
+                row_sum, total = block_sum, block
+            else:
+                decay = jnp.exp(row_max - new_max)
+                row_sum, total = row_sum * decay + block_sum, total * decay + block
+            row_max = new_max
+        part = head_rows(total * (1.0 / row_sum), head)
         result = part if result is None else result + part
         log_total[0, head : head + 1, :] = row_max + jnp.log(row_sum)
-    mixed[...] = jnp.transpose(result).astype(BF16)
+    result = jnp.transpose(result)
+    exact[...] = result
+    mixed[...] = result.astype(BF16)
 
 
 def attend_back_kernel(
@@ -290,35 +399,48 @@
     query_places,
     log_total,
     grad_mixed,
+    exact,
     grads,
     grad_keys,
     grad_values,
     k_turned,
+    marked,
 ):
     pair, tile = pl.program_id(0), pl.program_id(1)
     pairs, tiles = pl.num_programs(0), pl.num_programs(1)
     size = q.shape[0]
+    heads = LANES // HEAD
 
     @pl.when(tile == 0)
     def clear():
         grad_keys[...] = jnp.zeros_like(grad_keys)
         grad_values[...] = jnp.zeros_like(grad_values)
         k_turned[...] = turned(k[...])
-
-    mask = allowed(causal, key_docs, query_docs, key_places, query_places)
+        for head in range(heads):
+            marked[head] = marked_keys(k[...], key_docs[...], head)
+
     queries = q[...] * jnp.asarray(SCALE, BF16)
+    along = jnp.transpose(grad_mixed[...].astype(F32) * exact[...])
     grad_queries = None
-    for head in range(LANES // HEAD):
+    for head in range(heads):
         head_queries = in_head(queries, head)
+        searched = marked_queries(queries, query_docs[...], head)
         head_grad = in_head(grad_mixed[...], head)
-        scores = jnp.where(mask, inner(k[...], head_queries, 1, 1), MASK_VALUE)
-        attention = jnp.exp(scores - log_total[0, head : head + 1, :])
-        grad_attention = inner(v[...], head_grad, 1, 1)
-        row_delta = jnp.sum(attention * grad_attention, axis=0, keepdims=True)
-        grad_scores = (attention * (grad_attention - row_delta)).astype(BF16)
-        grad_values[...] += inner(attention.astype(BF16), head_grad, 1, 0)
-        grad_keys[...] += inner(grad_scores, head_queries, 1, 0)
-        part = head_rows(inner(k_turned[...], grad_scores, 1, 0), head)
+        row_delta = jnp.sum(along[head * HEAD : (head + 1) * HEAD], axis=0, keepdims=True)
+        row_log = log_total[0, head : head + 1, :]
+        total = None
+        for rows in blocked(k.shape[0]):
+            scores = inner(marked[head, rows, :], searched, 1, 1)
+            if causal:
+                scores = jnp.where(key_places[rows, :] <= query_places[...], scores, MASK_VALUE)
+            attention = jnp.exp(scores - row_log)
+            grad_attention = inner(v[rows, :], head_grad, 1, 1)
+            grad_scores = (attention * (grad_attention - row_delta)).astype(BF16)
+            grad_values[rows, :] += inner(attention.astype(BF16), head_grad, 1, 0)
+            grad_keys[rows, :] += inner(grad_scores, head_queries, 1, 0)
+            block = inner(k_turned[:, rows], grad_scores, 1, 0)
+            total = block if total is None else total + block
+        part = head_rows(total, head)
         grad_queries = part if grad_queries is None else grad_queries + part
 
     def column(block):
@@ -340,12 +462,13 @@
 
     row = pl.BlockSpec((1, tile), lambda p, i: (0, first + i))
     column = pl.BlockSpec((rows, 1), lambda p, i: (0, 0))
+    docs = pl.BlockSpec((tile, 1), lambda p, i: (first + i, 0))
     return [
         pl.BlockSpec((tile, LANES), lambda p, i: (first + i, offsets[0] + p)),
         keys(offsets[1]),
         keys(offsets[2]),
         column,
-        row,
+        docs,
         column,
         row,
     ]
@@ -354,73 +477,84 @@
 VMEM_BYTES = 48 * 1024 * 1024
 
 
-def attend_call(arrays, offsets, meta, causal, part, start, count):
+def attend_call(arrays, offsets, meta, causal, part, start, count, early=()):
     rows = arrays[0].shape[0]
     pairs, tile = part // LANES, min(count, 256)
     places = [offset // LANES for offset in offsets]
     return pl.pallas_call(
-        functools.partial(attend_kernel, causal),
+        without(functools.partial(attend_kernel, causal), 7, len(early)),
         grid=(pairs, count // tile),
-        in_specs=attend_specs(rows, tile, places, start // tile),
+        in_specs=attend_specs(rows, tile, places, start // tile)
+        + [pl.BlockSpec(memory_space=pl.ANY)] * len(early),
         out_specs=[
+            pl.BlockSpec((tile, LANES), lambda p, i: (i, p)),
             pl.BlockSpec((tile, LANES), lambda p, i: (i, p)),
             pl.BlockSpec((1, LANES // HEAD, tile), lambda p, i: (p, 0, i)),
         ],
         out_shape=[
             jax.ShapeDtypeStruct((count, part), BF16),
+            jax.ShapeDtypeStruct((count, part), F32),
             jax.ShapeDtypeStruct((pairs, LANES // HEAD, count), F32),
         ],
-        scratch_shapes=[pltpu.VMEM((LANES, rows), BF16)],
+        scratch_shapes=[
+            pltpu.VMEM((LANES, rows), BF16),
+            pltpu.VMEM((LANES // HEAD, rows, LANES), BF16),
+        ],
         compiler_params=pltpu.CompilerParams(vmem_limit_bytes=VMEM_BYTES),
-        cost_estimate=pl.CostEstimate(flops=0, bytes_accessed=0, transcendentals=0),
+        cost_estimate=pl.CostEstimate(flops=int(6e10), bytes_accessed=0, transcendentals=0),
         name="attend",
-    )(*arrays, *meta)
-
-
-def attend_back_call(arrays, offsets, meta, causal, part, log_total, grad_mixed):
+    )(*arrays, *meta, *early)
+
+
+def attend_back_call(arrays, offsets, meta, causal, part, stored, grad_mixed, early):
+    log_total, exact = stored
     rows = arrays[0].shape[0]
     pairs, tile = part // LANES, min(rows, 256)
     places = [offset // LANES for offset in offsets]
     return pl.pallas_call(
-        functools.partial(attend_back_kernel, causal),
+        without(functools.partial(attend_back_kernel, causal), 10, len(early)),
         grid=(pairs, rows // tile),
         in_specs=attend_specs(rows, tile, places, 0)
         + [
             pl.BlockSpec((1, LANES // HEAD, tile), lambda p, i: (p, 0, i)),
             pl.BlockSpec((tile, LANES), lambda p, i: (i, p)),
-        ],
+            pl.BlockSpec((tile, LANES), lambda p, i: (i, p)),
+        ]
+        + [pl.BlockSpec(memory_space=pl.ANY)] * len(early),
         out_specs=pl.BlockSpec((rows, 3 * part), lambda p, i: (0, 0)),
         out_shape=jax.ShapeDtypeStruct((rows, 3 * part), BF16),
         scratch_shapes=[
             pltpu.VMEM((rows, LANES), F32),
             pltpu.VMEM((rows, LANES), F32),
             pltpu.VMEM((LANES, rows), BF16),
+            pltpu.VMEM((LANES // HEAD, rows, LANES), BF16),
         ],
         compiler_params=pltpu.CompilerParams(vmem_limit_bytes=VMEM_BYTES),
-        cost_estimate=pl.CostEstimate(flops=0, bytes_accessed=0, transcendentals=0),
+        cost_estimate=pl.CostEstimate(flops=int(0), bytes_accessed=0, transcendentals=0),
         name="attend_back",
-    )(*arrays, *meta, log_total, grad_mixed)
-
-
-def layout_call(kernel, outs, name, tables, arrays):
+    )(*arrays, *meta, log_total, grad_mixed, exact, *early)
+
+
+def layout_call(kernel, outs, name, tables, arrays, early):
     whole = pl.BlockSpec(memory_space=pltpu.VMEM)
     return pl.pallas_call(
         kernel,
         grid_spec=pltpu.PrefetchScalarGridSpec(
             num_scalar_prefetch=len(tables),
             grid=(),
-            in_specs=[whole] * len(arrays),
+            in_specs=[whole] * len(arrays) + [pl.BlockSpec(memory_space=pl.ANY)] * len(early),
             out_specs=[whole] * len(outs),
         ),
         out_shape=outs,
         compiler_params=pltpu.CompilerParams(vmem_limit_bytes=VMEM_BYTES),
-        cost_estimate=pl.CostEstimate(flops=0, bytes_accessed=0, transcendentals=0),
+        cost_estimate=pl.CostEstimate(flops=int(6e10), bytes_accessed=0, transcendentals=0),
         name=name,
-    )(*tables, *arrays)
-
-
-def place(gathered, rows_at, outs, moves):
+    )(*tables, *arrays, *early)
+
+
+def place(gathered, rows_at, outs, moves, early=()):
     def kernel(rows_ref, source, *targets):
+        targets = targets[len(early) :]
         columns = source.shape[2]
         for out, row, column, k, first, count in moves:
             targets[out][row : row + count, column : column + columns] = source[
@@ -428,7 +562,7 @@
             ]
 
     shapes = [jax.ShapeDtypeStruct(shape, gathered.dtype) for shape in outs]
-    return layout_call(kernel, shapes, "place", [rows_at], [gathered])
+    return layout_call(kernel, shapes, "place", [rows_at], [gathered], early)
 
 
 def fold(matrix, columns):
@@ -466,15 +600,19 @@
     part = width // G
     hid = hidden_share * K
 
-    def to_row(embed):
+    def to_row(embed, *early):
         got = []
         for k in range(micro):
             message = jnp.where((grid.b ^ k) == 0, embed[0, 0], embed[1, 0])
+            if early:
+                message = gate(message, *early)
             got.append(grid.send(message, lambda r, c, a, i, b: (r, a, b ^ k, i, c)))
         return jnp.where(grid.a == 0, jnp.concatenate(got), jnp.concatenate(got[::-1])).astype(F32)
 
-    def from_row(gradient):
+    def from_row(gradient, *early):
         gradient = gradient.astype(BF16)
+        if early:
+            gradient = gate(gradient, *early)
         got = []
         for k in range(micro):
             message = jnp.where((grid.a ^ k) == 0, gradient[:tokens], gradient[tokens:])
@@ -486,10 +624,11 @@
     def member_rows(k, member):
         return grid.flat(k // 4, member // I, k // 2 % 2, member % I, k % 2) * share
 
-    def natural_in(found):
+    def natural_in(found, early=()):
         gathered, rows_at = found
         if not kernels:
-            gathered = jnp.take(gathered, rows_at, axis=0).reshape(R, 2, 2, 2, I, 3, share, part)
+            gathered = jnp.take(gathered, rows_at, axis=0)[:, : G * 3 * share]
+            gathered = gathered.reshape(R, 2, 2, 2, I, 3, share, part)
             return gathered.transpose(0, 3, 1, 4, 2, 6, 5, 7).reshape(width, 3 * part)
         moves = [
             (0, member_rows(k, member), j * part, k, (member * 3 + j) * share, share)
@@ -497,7 +636,7 @@
             for member in range(G)
             for j in range(3)
         ]
-        return place(gathered, rows_at, [(width, 3 * part)], moves)[0]
+        return place(gathered, rows_at, [(width, 3 * part)], moves, early)[0]
 
     def natural_out(found):
         gathered, rows_at = found
@@ -516,10 +655,13 @@
     def in_blocks(weight):
         return weight.reshape(-1, G, part).transpose(1, 0, 2)
 
-    first = grid.exchange(in_blocks(attend_in[0].reshape(3 * share, width)))
-    in_0 = Gathering(grid, first.reshape(-1, part), "abr")
+    first = in_blocks(attend_in[:2].reshape(6 * share, width))
+    source_embed, unused = lax.optimization_barrier((source_embed, first))
+    first = grid.exchange(first)
+    in_0 = Gathering(grid, first[:, : 3 * share].reshape(-1, part), "abr")
     in_0.step()
     source = to_row(source_embed)
+    norm_gain = tie(norm_gain, first)
 
     small = jnp.concatenate(
         [
@@ -577,45 +719,45 @@
         .astype(jnp.int32)
     )
 
-    later_in, feed_up, target_embed, attend_out, unused = lax.optimization_barrier(
-        (attend_in[1:], feed_up, target_embed, attend_out, in_0.gathered)
-    )
+    in_0.step()
+    attend_out, feed_up, unused = lax.optimization_barrier((attend_out, feed_up, in_0.gathered))
     out_piece = grid.send(
         attend_out, lambda r, c, a, i, b: out_home(grid.flat(r, c, a, i, b))
     ).reshape(3 * share, width)
     ups = feed_up.reshape(2 * share, R, 2, 2, I, 2, hidden_share)
-    ups = grid.exchange(ups.transpose(2, 4, 0, 1, 3, 5, 6).reshape(G, 2 * share, hid))
-    later_in = grid.exchange(in_blocks(later_in.reshape(6 * share, width)))
-    target = to_row(target_embed)
-
-    def in_bundle(which):
-        return later_in[:, (which - 1) * 3 * share : which * 3 * share].reshape(-1, part)
+    ups = ups.transpose(2, 4, 0, 1, 3, 5, 6).reshape(G, 2 * share, hid)
+    ups = grid.exchange(ups)
+    blocks_2 = grid.exchange(in_blocks(attend_in[2].reshape(3 * share, width)))
+    folds = hid // part
 
     def feed_bundle(which):
         up = ups[:, which * share : (which + 1) * share].reshape(-1, hid)
         return jnp.concatenate([up, fold(feed_down[which], hid)])
 
-    def feed_weights(found):
+    def feed_weights(found, start=0, count=1, early=()):
         gathered, rows_at = found
-        folds = width // hid
+        tall = G * share + hidden_share * width // hid
         if not kernels:
-            gathered = jnp.take(gathered, rows_at, axis=0)
+            gathered = jnp.take(gathered, rows_at, axis=0)[:, start:]
+            gathered = unfold(gathered, tall)
             up = gathered[:, : G * share].reshape(R, 2, 2, 2, I, share, hid)
             down = unfold(gathered[:, G * share :], hidden_share)
             return up.transpose(0, 3, 1, 4, 2, 5, 6).reshape(width, hid), down.reshape(hid, width)
-        moves = [
-            (0, member_rows(k, member), 0, k, member * share, share)
-            for k in range(K)
-            for member in range(G)
-        ]
-        for k in range(K):
-            for j in range(folds):
-                row = G * share + j * hidden_share
-                moves.append((1, k * hidden_share, j * hid, k, row, hidden_share))
-        return place(gathered, rows_at, [(width, hid), (hid, width)], moves)
+        moves = []
+        for block in range(count):
+            column, base = block * (hid // count), start + block * tall
+            for k in range(K):
+                for member in range(G):
+                    first_row = base + member * share
+                    moves.append((0, member_rows(k, member), column, k, first_row, share))
+                for j in range(width // hid):
+                    row = base + G * share + j * hidden_share
+                    target = j * hid + column
+                    moves.append((1, k * hidden_share, target, k, row, hidden_share))
+        return place(gathered, rows_at, [(width, hid), (hid, width)], moves, early)
 
     def meta(query_docs, key_docs):
-        return (key_docs[:, None], query_docs[None, :], places[:, None], places[None, :])
+        return (key_docs[:, None], query_docs[:, None], places[:, None], places[None, :])
 
     source_meta = meta(source_row_docs, source_row_docs)
     target_meta = meta(target_row_docs, target_row_docs)
@@ -644,8 +786,10 @@
         chips, results = apply_far(launched, apply)
         return [near] + chips, [near_result] + results
 
-    def send_far(parts):
-        joints = [order.did(grid.join_cores(array)) for array in parts]
+    def send_far(parts, *early):
+        joints = [grid.join_cores(array).astype(BF16) for array in parts]
+        if early:
+            joints[0] = gate(joints[0], *early)
         return [grid.return_chip(joint, k + 1) for k, joint in enumerate(joints)]
 
     def receive(near_part, sent):
@@ -654,25 +798,27 @@
             total = total + order.use(array).astype(F32)
         return total
 
-    def attend_far(arrays, offsets, meta_rows, causal):
-        held = order.use(arrays[0])
-        arrays = [held if array is arrays[0] else array for array in arrays]
-        far = attend_call(arrays, offsets, meta_rows, causal, part, chip, rows - chip)
-        order.did(far[0])
-        return far
-
-    def attend_near(arrays, offsets, meta_rows, causal):
-        held = order.use(arrays[0])
-        arrays = [held if array is arrays[0] else array for array in arrays]
-        near = attend_call(arrays, offsets, meta_rows, causal, part, 0, chip)
-        order.did(near[0])
-        return near
+    def attend_all(arrays, offsets, meta_rows, causal, early):
+        mixed, exact, log_total = attend_call(
+            arrays, offsets, meta_rows, causal, part, 0, rows, early
+        )
+        order.did(mixed)
+        return [mixed[k * chip : (k + 1) * chip] for k in range(I)], (log_total, exact)
+
+    def attend_far(arrays, offsets, meta_rows, causal, early=()):
+        return attend_call(
+            arrays, offsets, meta_rows, causal, part, chip, rows - chip, early
+        )
+
+    def attend_near(arrays, offsets, meta_rows, causal, early=()):
+        return attend_call(arrays, offsets, meta_rows, causal, part, 0, chip, early)
 
     def by_far_chip(array):
         return [array[k * chip : (k + 1) * chip] for k in range(I - 1)]
 
     def stored(near, far):
-        return [near[0]] + by_far_chip(far[0]), jnp.concatenate([near[1], far[1]], axis=2)
+        kept = (jnp.concatenate([near[2], far[2]], axis=2), jnp.concatenate([near[1], far[1]]))
+        return [near[0]] + by_far_chip(far[0]), kept
 
     def far_product(array, weight):
         return [product(order.use(p), weight) for p in by_far_chip(array)]
@@ -691,72 +837,65 @@
     cross_offsets = (0, 0, part)
 
     out_all = Gathering(grid, out_piece, "arb")
-    feed_0 = Gathering(grid, feed_bundle(0), "abr")
-    in_1 = Gathering(grid, in_bundle(1), "arb")
-    in_2 = Gathering(grid, in_bundle(2), "abr")
-    feed_1 = Gathering(grid, feed_bundle(1), "arb")
-
+    in_1 = Gathering(grid, first[:, 3 * share :].reshape(-1, part), "arb")
+    in_order = jnp.arange(K, dtype=jnp.int32)
     enc_start = layer_norm(source, gains[0], biases[0])
     enc_normed = layer_norm(enc_start, gains[1], biases[1]).astype(BF16)
     in_0.step()
-    out_all.step(in_0.gathered)
-    in_0.step()
+    out_all.step()
+    in_1.step()
+    feed_0 = Gathering(grid, feed_bundle(0), "abr")
+    feed_0.step()
     enc_launched = launch(enc_normed)
+    w_in_0 = natural_in(in_0.finish())
+    enc_in, results = apply_all(enc_launched, projection(w_in_0))
+    enc_qkv = jnp.concatenate(results)
+    out_all.step()
+    in_1.step()
+    target = to_row(target_embed, w_in_0)
     dec_start = layer_norm(target, gains[4], biases[4])
     dec_normed = layer_norm(dec_start, gains[5], biases[5]).astype(BF16)
-    feed_0.step(out_all.gathered)
-    out_all.step(in_0.gathered)
-    in_1.step(in_0.gathered)
-    w_in_0 = order.did(natural_in(in_0.finish(dec_normed)))
-    enc_in, results = apply_all(enc_launched, projection(w_in_0))
-    enc_qkv = jnp.concatenate(results)
-    in_1.step(order.last)
-    feed_0.step(order.last)
-    out_all.step(order.last)
+    dec_launched = launch(dec_normed)
+    fed = feed_0.step()
     enc_source = ([enc_qkv] * 3, self_offsets, source_meta, False)
-    far = attend_far(*enc_source)
-    near = attend_near(*enc_source)
-    feed_0.step(order.last)
-    in_1.step(order.last)
-    dec_launched = launch(dec_normed)
-    w_out = natural_out(out_all.finish(order.last))
+    far = attend_far(*enc_source, [fed])
+    out_all.step()
+    w_out = natural_out(out_all.finish())
+    sent = send_far(far_product(far[0], w_out[0]))
+    in_2 = Gathering(grid, blocks_2.reshape(-1, part), "abr")
+    feed_1 = Gathering(grid, feed_bundle(1), "arb")
+    near = attend_near(*enc_source, [in_2.step(), feed_1.step()])
     enc_mixed, enc_log = stored(near, far)
-    sent = send_far(far_product(far[0], w_out[0]))
-    in_2.step(order.last)
-    near_part = product(order.use(near[0]), w_out[0])
-    w_in_1 = order.did(natural_in(in_1.finish(order.last)))
+    in_1.step()
+    w_in_1 = natural_in(in_1.finish())
+    enc_near = product(near[0], w_out[0])
     dec_in, results = apply_all(dec_launched, projection(w_in_1))
     dec_qkv = jnp.concatenate(results)
-    enc_middle = order.did(enc_start + receive(near_part, sent))
+    dec_source = ([dec_qkv] * 3, self_offsets, target_meta, True)
+    enc_middle = enc_start + receive(enc_near, sent)
     ff_normed = layer_norm(enc_middle, gains[2], biases[2]).astype(BF16)
-    enc_launched = launch(order.did(ff_normed))
-    in_2.step(order.last)
-    feed_1.step(order.last)
-    dec_source = ([dec_qkv] * 3, self_offsets, target_meta, True)
-    far = attend_far(*dec_source)
+    enc_launched = launch(ff_normed)
+    fed = feed_0.step()
+    far = attend_far(*dec_source, [fed, in_2.step()])
     sent = send_far(far_product(far[0], w_out[1]))
-    near = attend_near(*dec_source)
+    near = attend_near(*dec_source, [feed_1.step(), in_2.step()])
     dec_mixed, dec_log = stored(near, far)
-    near_part = product(near[0], w_out[1])
-    up_0, down_0 = feed_weights(feed_0.finish(near_part))
-    feed_1.step(near_part)
-    in_2.step(near_part)
-    dec_self = order.did(dec_start + receive(near_part, sent))
+    dec_self = dec_start + receive(product(near[0], w_out[1]), sent)
     cross_normed = layer_norm(dec_self, gains[6], biases[6]).astype(BF16)
+    up_0, down_0 = feed_weights(feed_0.finish(), early=[feed_1.step()])
     ff_chips_0, hidden_0 = apply_all(enc_launched, rise(up_0))
     sent = send_far([product(h, down_0) for h in hidden_0[1:]])
     cross_launched = launch(cross_normed)
     enc_end = enc_middle + receive(product(order.use(hidden_0[0]), down_0), sent)
     encoded = order.did(layer_norm(enc_end, gains[3], biases[3]).astype(BF16))
     encoded_launched = launch(encoded)
-    w_in_2 = natural_in(in_2.finish(order.last))
+    w_in_2 = natural_in(in_2.finish())
     cross_w_q, cross_w_kv = w_in_2[:, :part], w_in_2[:, part:]
     cross_in, results = apply_all(cross_launched, projection(cross_w_q))
     cross_q = jnp.concatenate(results)
     encoded_in, results = apply_all(encoded_launched, projection(cross_w_kv))
     cross_kv = jnp.concatenate(results)
     cross_source = ([cross_q, cross_kv, cross_kv], cross_offsets, cross_meta, False)
-    feed_1.step(order.last)
     far = attend_far(*cross_source)
     sent = send_far(far_product(far[0], w_out[2]))
     near = attend_near(*cross_source)
@@ -764,7 +903,7 @@
     dec_cross = dec_self + receive(product(near[0], w_out[2]), sent)
     ff_normed = order.did(layer_norm(dec_cross, gains[7], biases[7]).astype(BF16))
     dec_launched = launch(ff_normed)
-    up_1, down_1 = feed_weights(feed_1.finish(order.last))
+    up_1, down_1 = feed_weights(feed_1.finish())
     ff_chips_1, hidden_1 = apply_all(dec_launched, rise(up_1))
     sent = send_far([product(h, down_1) for h in hidden_1[1:]])
     dec_end = dec_cross + receive(product(order.use(hidden_1[0]), down_1), sent)
@@ -811,8 +950,8 @@
         )
         return order.did(rows_inner(left, right).astype(BF16))
 
-    def far_back(grads, weight):
-        return send_far([by_transpose(order.use(g), weight) for g in grads[1:]])
+    def far_back(grads, weight, *early):
+        return send_far([by_transpose(g, weight) for g in grads[1:]], *early)
 
     def near_back(grads, weight):
         return order.did(by_transpose(order.use(grads[0]), weight))
@@ -827,45 +966,52 @@
     def back_projection(weight):
         return lambda grad, unused: by_transpose(grad, weight).astype(BF16)
 
-    def attend_back(source, log_total, grad_mixed):
+    def attend_back(source, kept, grad_mixed, early=()):
         arrays, offsets, meta_rows, causal = source
-        grad_mixed = order.use(jnp.concatenate(grad_mixed))
-        return order.did(
-            attend_back_call(arrays, offsets, meta_rows, causal, part, log_total, grad_mixed)
+        grad_mixed = jnp.concatenate(grad_mixed)
+        return attend_back_call(
+            arrays, offsets, meta_rows, causal, part, kept, grad_mixed, early
         )
 
     def by_chip(matrix):
         return [matrix[i * chip : (i + 1) * chip] for i in range(I)]
 
-    def feed_scatter(up_grad, down_grad, name):
+    def feed_bundle_grad(up_grad, down_grad):
         up_grad = up_grad.reshape(R, 2, 2, I, 2, share, hid)
-        up_grad = up_grad.transpose(0, 2, 4, 1, 3, 5, 6).reshape(R, 2, 2, G * share, hid)
-        down_grad = fold(down_grad.reshape(R, 2, 2, hidden_share, width), hid)
-        bundle = jnp.concatenate([up_grad, down_grad], axis=3)
-        return Scattering(grid, bundle, name, (0, 1, 2))
+        up_grad = up_grad.transpose(0, 2, 4, 1, 3, 5, 6).reshape(K, G * share, hid)
+        down_grad = fold(down_grad.reshape(K, hidden_share, width), hid)
+        return order.did(jnp.concatenate([up_grad, down_grad], axis=1))
+
+    def row_sum(bundle):
+        return lax.psum_scatter(bundle, ACROSS, scatter_dimension=0)
+
+    def feed_steps(bundle, name):
+        return Scattering(grid, bundle.reshape((R, 2, 2) + bundle.shape[1:]), name, (0, 1, 2))
 
     def settle_feed(total):
-        total = total[0, 0, 0]
         up = grid.exchange(total[: G * share].reshape(G, share, hid).astype(BF16))
         up = up.reshape(2, I, share, R, 2, 2, hidden_share).transpose(2, 3, 0, 4, 1, 5, 6)
-        return up.reshape(share, -1).astype(F32), unfold(total[G * share :], hidden_share)
+        return up.reshape(share, -1).astype(F32), unfold(total[G * share :].astype(F32), hidden_share)
 
     def in_scatter(grads, name):
         grads = grads.reshape(R, 2, 2, I, 2, share, 3 * part)
         return Scattering(grid, grads, name, (0, 2, 4))
 
+    def in_rows(grads):
+        grads = grads.reshape(R, 2, 2, I, 2, share, 3 * part).transpose(0, 2, 4, 1, 3, 5, 6)
+        return grads.reshape(K, G * share, 3 * part)
+
     def settle_in(total):
         total = grid.exchange(total.reshape(G, share, 3 * part).astype(BF16)).astype(F32)
         return total.reshape(G, share, 3, part).transpose(2, 1, 0, 3).reshape(3, share, width)
 
+    order.kept = True
     grad_dec_end = back_norm(dec_end, 8, grad_final)
     launched = launch(order.did(grad_dec_end.astype(BF16)))
     branch, grad_ups = apply_all(launched, fall(ff_chips_1, up_1, down_1))
     sent = far_back(grad_ups, up_1)
     near_part = near_back(grad_ups, up_1)
-    feed_1 = feed_scatter(
-        rows_sum(ff_chips_1, grad_ups), rows_sum(hidden_1, branch), "abr"
-    )
+    feed_1 = feed_steps(feed_bundle_grad(rows_sum(ff_chips_1, grad_ups), rows_sum(hidden_1, branch)), "abr")
     feed_1.step(order.last)
     grad_dec_cross = grad_dec_end + back_norm(dec_cross, 7, receive(near_part, sent))
 
@@ -891,9 +1037,7 @@
     enc_branch, grad_ups = apply_all(enc_launched, fall(ff_chips_0, up_0, down_0))
     sent = far_back(grad_ups, up_0)
     near_part = near_back(grad_ups, up_0)
-    feed_0 = feed_scatter(
-        rows_sum(ff_chips_0, grad_ups), rows_sum(hidden_0, enc_branch), "abr"
-    )
+    feed_0 = feed_steps(feed_bundle_grad(rows_sum(ff_chips_0, grad_ups), rows_sum(hidden_0, enc_branch)), "abr")
     feed_0.step(order.last)
     in_2.step(order.last)
     grad_enc_middle = grad_enc_end + back_norm(enc_middle, 2, receive(near_part, sent))
@@ -906,24 +1050,26 @@
     branch, grad_mixed = apply_all(enc_launched, back_projection(w_out[0]))
     sent_1 = far_back(by_chip(grads_1), w_in_1)
     grads_0 = attend_back(enc_source, enc_log, grad_mixed)
-    sent_0 = far_back(by_chip(grads_0), w_in_0)
+    in_0 = in_scatter(rows_sum(enc_in, grads_0), "abr")
+    given_0 = in_0.step()
+    sent_0 = far_back(by_chip(grads_0), w_in_0, given_0)
     near_0 = near_back(by_chip(grads_0), w_in_0)
     near_1 = near_back(by_chip(grads_1), w_in_1)
-    feed_0.step(order.last)
-    in_0 = in_scatter(rows_sum(enc_in, grads_0), "arb")
-    in_0.step(order.last)
-    in_1 = in_scatter(rows_sum(dec_in, grads_1), "abr")
-    in_1.step(order.last)
+    given = feed_0.step()
+    in_1 = in_scatter(rows_sum(dec_in, grads_1), "arb")
+    given_1 = in_1.step()
+    grad_dec_start = grad_dec_self + back_norm(dec_start, 5, receive(near_1, sent_1))
+    target_grad = from_row(back_norm(target, 4, grad_dec_start), given_1, given)
     grad_enc_start = grad_enc_middle + back_norm(enc_start, 1, receive(near_0, sent_0))
-    source_grad = from_row(order.did(back_norm(source, 0, grad_enc_start)))
-    grad_dec_start = grad_dec_self + back_norm(dec_start, 5, receive(near_1, sent_1))
-    target_grad = from_row(order.did(back_norm(target, 4, grad_dec_start)))
+    source_grad = from_row(back_norm(source, 0, grad_enc_start), in_0.step())
     outs = [rows_sum(enc_mixed, branch), rows_sum(dec_mixed, dec_branch), out_2]
     out_grads = jnp.concatenate([g.reshape(R, 2, 2, share, width) for g in outs], axis=3)
     out_all = Scattering(grid, out_grads, "abr", (0, 1, 2))
     out_all.step(order.last)
+    norm_grads = jnp.stack(gain_grads + bias_grads)
+    norm_grads = norm_grads.reshape(2 * norms, n, share).transpose(1, 0, 2)
+    norm_grads = lax.all_to_all(gate(norm_grads, in_0.step()), AXES, 0, 0)
     feed_0.step(order.last)
-    in_0.step(order.last)
     in_1.step(order.last)
 
     def out_owner(r, c, a, i, b):
@@ -936,16 +1082,14 @@
             block % 2,
         )
 
-    feed_1 = settle_feed(feed_1.finish())
+    feed_1 = settle_feed(feed_1.finish()[0, 0, 0])
     in_2 = settle_in(in_2.finish())
+    in_0 = settle_in(in_0.finish())
     in_1 = settle_in(in_1.finish())
-    feed_0 = settle_feed(feed_0.finish())
+    feed_0 = settle_feed(feed_0.finish()[0, 0, 0])
     attend_out_grad = grid.send(out_all.finish().reshape(3, share, width), out_owner)
-    in_0 = settle_in(in_0.finish())
-
-    norm_grads = jnp.stack(gain_grads + bias_grads)
-    norm_grads = norm_grads.reshape(2 * norms, n, share).transpose(1, 0, 2)
-    norm_grads = jnp.sum(lax.all_to_all(norm_grads, AXES, 0, 0), axis=0)
+
+    norm_grads = jnp.sum(norm_grads, axis=0)
 
     return (
         mean_loss,

time: 1020 us -> 999 us (0.979)
  blocking collectives: 41.1 us -> 12.2 us
  waiting for transfers between devices: 333 us -> 306 us
  starting transfers between devices: 168 us -> 188 us
  local copies, waits for them, and re-layouts: 114 us -> 127 us
    ppermute x112, waiting for transfers between devices: 286 us -> 254 us  [send(): return lax.ppermute(array, AXES, pairs)]
    all_to_all x1 -> x0, blocking collectives: 28.9 us -> none  [local(): grad_rows = lax.all_to_all(grad_rows.astype(BF16), AXES, 0, 0)]
    concatenate x26 -> x29, other arithmetic: 22.4 us -> 37.5 us  [the longest x18 33.5 us: land(): self.gathered = jnp.concatenate([self.gathered, self.got])]
    ppermute x112, starting transfers between devices: 114 us -> 126 us  [send(): return lax.ppermute(array, AXES, pairs)]
    add x26 -> x15, other arithmetic: 32.3 us -> 20.7 us  [land(): self.parts = self.keep.astype(F32) + self.got.astype(F32)]
    concatenate x22 -> x10, other arithmetic: 18.6 us -> 7.64 us  [both_cores(): return jnp.concatenate([array, self.swap_cores(array)])]
    pallas_call x9 -> x15, Pallas kernels: 101 us -> 93.5 us  [the longest x6 48.8 us: attend_call(): pl.pallas_call(without(functools.partial(attend_kernel, causal), 7, len(e...]
    all_to_all x1 -> x2, waiting for transfers between devices: 19.6 us -> 25.1 us  [the longest x1 20.9 us: local(): grad_rows = lax.all_to_all(grad_rows.astype(BF16), AXES, 0, 0)]
  transfers between devices with their start and end apart: 123 -> 124, of which waited for: 42 -> 37; matrix products, arithmetic and copies ran while one was open for 27% -> 31% of each run, Pallas kernels for 9% -> 10%
where the time goes in v2:
time: 999 us; the launch traced here: 987 us
  waiting for transfers between devices  306 us (31%)
  starting transfers between devices  188 us (19%)
  other arithmetic  159 us (16%)
  local copies, waits for them, and re-layouts  127 us (13%)
  Pallas kernels  102 us (10%)
  matrix products  84.9 us (8%)
  blocking collectives  12.2 us (1%)
    ppermute x112, waiting for transfers between devices, send(): return lax.ppermute(array, AXES, pairs)  254 us
    ppermute x112, starting transfers between devices, send(): return lax.ppermute(array, AXES, pairs)  126 us
    pallas_call x6, Pallas kernels, attend_call(): pl.pallas_call(without(functools.partial(attend_kernel, causal), 7, len(e...  48.8 us
    pallas_call x3, Pallas kernels, attend_back_call(): pl.pallas_call(without(functools.partial(attend_back_kernel, causal), 10,...  44.7 us
    all_to_all x8, starting transfers between devices, exchange(): return lax.all_to_all(blocks, MEMBERS, 0, 0)  43.2 us
    unnamed x612, local copies, waits for them, and re-layouts  39.3 us
    dot_general x23, matrix products, product(): return jnp.dot(left, right, preferred_element_type=F32)  34.4 us
    concatenate x18, other arithmetic, land(): self.gathered = jnp.concatenate([self.gathered, self.got])  33.5 us
  transfers between devices with their start and end apart: 124, of which 37 were waited for; matrix products, arithmetic and copies ran while one was open for 31% of the time, Pallas kernels for 10%

profile of v2, /device:TPU:8, one launch (start us, length us, event | category | flops | bytes accessed | tf_op | source)
XLA Modules:
  0.0 986.7 jit_solution(9429053631150934452)
XLA Ops:
  99.9 10.9 %collective-permute-done.15 = bf16[1,96,1024]{2,1,0:T(8,128)(2,1)S(1)} collective-permute-done((bf16[1,96,1024]{2,1,0:T(8,128)(2,1)}, bf16[1,96,1024]{2,1,0:T(8,128)(2,1)S(1)}, u32[]{:S(2)}, u32[]{:S(2)}) %collective-permute-start.15) | collective-permute-done | bytes 196640 | tf_op jit(solution)/shard_map/ppermute | solution.py:90
  120.3 7.8 collective-permute-done.16
  148.8 8.0 attend.8
  157.7 11.6 %collective-permute-done.19 = bf16[1,256,1024]{2,1,0:T(8,128)(2,1)} collective-permute-done((bf16[1,256,1024]{2,1,0:T(8,128)(2,1)}, bf16[1,256,1024]{2,1,0:T(8,128)(2,1)}, u32[]{:S(2)}, u32[]{:S(2)}) %collective-permute-start.19) | collective-permute-done | bytes 524320 | tf_op jit(solution)/shard_map/ppermute | solution.py:90
  170.6 8.1 attend.9
  217.8 8.4 attend.6
  227.0 8.0 attend.7
  240.8 11.6 %collective-permute-done.39 = bf16[256,1024]{1,0:T(8,128)(2,1)S(1)} collective-permute-done((bf16[256,1024]{1,0:T(8,128)(2,1)S(1)}, bf16[256,1024]{1,0:T(8,128)(2,1)S(1)}, u32[]{:S(2)}, u32[]{:S(2)}) %collective-permute-start.39) | collective-permute-done | bytes 524320 | tf_op jit(solution)/shard_map/ppermute | solution.py:90
  252.7 12.8 %collective-permute-done.36 = bf16[4,256,1024]{2,1,0:T(8,128)(2,1)} collective-permute-done((bf16[4,256,1024]{2,1,0:T(8,128)(2,1)S(1)}, bf16[4,256,1024]{2,1,0:T(8,128)(2,1)}, u32[]{:S(2)}, u32[]{:S(2)}) %collective-permute-start.36) | collective-permute-done | bytes 2097184 | tf_op jit(solution)/shard_map/ppermute | solution.py:90
  290.1 11.1 %collective-permute-done.42 = bf16[256,1024]{1,0:T(8,128)(2,1)S(1)} collective-permute-done((bf16[256,1024]{1,0:T(8,128)(2,1)S(1)}, bf16[256,1024]{1,0:T(8,128)(2,1)S(1)}, u32[]{:S(2)}, u32[]{:S(2)}) %collective-permute-start.42) | collective-permute-done | bytes 524320 | tf_op jit(solution)/shard_map/ppermute | solution.py:90
  305.7 11.8 %collective-permute-done.25 = bf16[256,1024]{1,0:T(8,128)(2,1)S(1)} collective-permute-done((bf16[256,1024]{1,0:T(8,128)(2,1)S(1)}, bf16[256,1024]{1,0:T(8,128)(2,1)S(1)}, u32[]{:S(2)}, u32[]{:S(2)}) %collective-permute-start.25) | collective-permute-done | bytes 524320 | tf_op jit(solution)/shard_map/ppermute | solution.py:90
  320.0 7.7 collective-permute-done.44
  331.6 8.1 attend.11
  340.7 8.2 attend.10
  354.7 12.6 %collective-permute-done.48 = bf16[256,1024]{1,0:T(8,128)(2,1)} collective-permute-done((bf16[256,1024]{1,0:T(8,128)(2,1)}, bf16[256,1024]{1,0:T(8,128)(2,1)}, u32[]{:S(2)}, u32[]{:S(2)}) %collective-permute-start.48) | collective-permute-done | bytes 524320 | tf_op jit(solution)/shard_map/ppermute | solution.py:90
  402.1 12.3 %collective-permute-done.55 = bf16[256,1024]{1,0:T(8,128)(2,1)S(1)} collective-permute-done((bf16[256,1024]{1,0:T(8,128)(2,1)S(1)}, bf16[256,1024]{1,0:T(8,128)(2,1)S(1)}, u32[]{:S(2)}, u32[]{:S(2)}) %collective-permute-start.55) | collective-permute-done | bytes 524320 | tf_op jit(solution)/shard_map/ppermute | solution.py:90
  424.4 25.8 %all-to-all-done.4 = bf16[32,12,1024]{2,1,0:T(8,128)(2,1)} async-done(((bf16[32,12,1024]{2,1,0:T(8,128)(2,1)}), bf16[32,12,1024]{2,1,0:T(8,128)(2,1)}, u32[]{:S(2)}, u32[]{:S(2)}) %all-to-all-start.4) | async-done | bytes 786464 | tf_op jit(solution)/shard_map/all_to_all | solution.py:93
  455.1 12.2 %all_to_all.69 = f32[32,3,384]{2,1,0:T(4,128)S(1)} all-to-all(f32[32,3,384]{2,1,0:T(4,128)S(1)} %broadcast_in_dim.29), channel_id=1, replica_groups=mesh['r'=2,'c'=2,'a'=2,'i'=2,'b'=2] {'r','c','a','i','b'}, dimensions={0} | all-to-all | bytes 294912 | tf_op jit(solution)/shard_map/all_to_all | solution.py:93
  480.8 20.9 %all-to-all-done.6 = bf16[32,12,1024]{2,1,0:T(8,128)(2,1)} async-done(((bf16[32,12,1024]{2,1,0:T(8,128)(2,1)}), bf16[32,12,1024]{2,1,0:T(8,128)(2,1)}, u32[]{:S(2)}, u32[]{:S(2)}) %all-to-all-start.6) | async-done | bytes 786464 | tf_op jit(solution)/shard_map/all_to_all | solution.py:936
  517.3 10.1 %collective-permute-done.57 = bf16[256,1024]{1,0:T(8,128)(2,1)S(1)} collective-permute-done((bf16[256,1024]{1,0:T(8,128)(2,1)S(1)}, bf16[256,1024]{1,0:T(8,128)(2,1)S(1)}, u32[]{:S(2)}, u32[]{:S(2)}) %collective-permute-start.57) | collective-permute-done | bytes 524320 | tf_op jit(solution)/shard_map/ppermute | solution.py:90
  549.3 9.2 collective-permute-done.61
  568.8 10.6 %collective-permute-done.63 = bf16[256,1024]{1,0:T(8,128)(2,1)S(1)} collective-permute-done((bf16[256,1024]{1,0:T(8,128)(2,1)S(1)}, bf16[256,1024]{1,0:T(8,128)(2,1)S(1)}, u32[]{:S(2)}, u32[]{:S(2)}) %collective-permute-start.63) | collective-permute-done | bytes 524320 | tf_op jit(solution)/shard_map/ppermute | solution.py:90
  579.4 16.8 %collective-permute-done.109 = bf16[1,2,2,256,1024]{4,3,2,1,0:T(8,128)(2,1)S(1)} collective-permute-done((bf16[1,2,2,256,1024]{4,3,2,1,0:T(8,128)(2,1)S(1)}, bf16[1,2,2,256,1024]{4,3,2,1,0:T(8,128)(2,1)S(1)}, u32[]{:S(2)}, u32[]{:S(2)}) %collective-permute-start.109) | collective-permute-done | bytes 2097184 | tf_op jit(solution)/shard_map/ppermute | solution.py:90
  601.2 15.5 %attend_back.3 = bf16[1024,768]{1,0:T(8,128)(2,1)} custom-call(bf16[1024,256]{1,0:T(8,128)(2,1)S(1)} %copy-done.24, bf16[1024,512]{1,0:T(8,128)(2,1)S(1)} %pad_maximum_fusion.29.refs_1_.refs_2_, bf16[1024,512]{1,0:T(8,128)(2,1)S(1)} %pad_maximum_fusion.29.refs_1_.refs_2_, s32[1024,1]{1,0:T(8,128)S(1)} %copy-done.11, s32[1024,1]{1,0:T(8,128)S(1)} %copy-done.15, ...), custom_call_target="tpu_custom_call" | custom-call | tf_op jit(solution)/shard_map/attend_back/pallas_call | solution.py:514
  630.3 19.0 %collective-permute-done.67 = bf16[256,1024]{1,0:T(8,128)(2,1)S(1)} collective-permute-done((bf16[256,1024]{1,0:T(8,128)(2,1)S(1)}, bf16[256,1024]{1,0:T(8,128)(2,1)S(1)}, u32[]{:S(2)}, u32[]{:S(2)}) %collective-permute-start.67) | collective-permute-done | bytes 524320 | tf_op jit(solution)/shard_map/ppermute | solution.py:90
  713.9 7.3 collective-permute-done.76
  756.7 9.2 collective-permute-done.81
  766.0 14.9 %attend_back.5 = bf16[1024,768]{1,0:T(8,128)(2,1)S(1)} custom-call(bf16[1024,768]{1,0:T(8,128)(2,1)S(1)} %copy-done.4, bf16[1024,768]{1,0:T(8,128)(2,1)S(1)} %copy-done.4, bf16[1024,768]{1,0:T(8,128)(2,1)S(1)} %copy-done.4, s32[1024,1]{1,0:T(8,128)S(1)} %copy-done.16, s32[1024,1]{1,0:T(8,128)S(1)} %copy-done.16, s32[1024,1]{1,0:T(8,128)S(1)} %copy-done.8, ...), custom_call_target="tpu_custom_call" | custom-call | tf_op jit(solution)/shard_map/attend_back/pallas_call | solution.py:514
  795.4 14.3 %attend_back.4 = bf16[1024,768]{1,0:T(8,128)(2,1)S(1)} custom-call(bf16[1024,768]{1,0:T(8,128)(2,1)S(1)} %copy-done.2, bf16[1024,768]{1,0:T(8,128)(2,1)S(1)} %copy-done.2, bf16[1024,768]{1,0:T(8,128)(2,1)S(1)} %copy-done.2, s32[1024,1]{1,0:T(8,128)S(1)} %copy-done.12, s32[1024,1]{1,0:T(8,128)S(1)} %copy-done.12, s32[1024,1]{1,0:T(8,128)S(1)} %copy-done.8, ...), custom_call_target="tpu_custom_call" | custom-call | tf_op jit(solution)/shard_map/attend_back/pallas_call | solution.py:514
  831.9 12.8 %collective-permute-done.91 = bf16[256,1024]{1,0:T(8,128)(2,1)} collective-permute-done((bf16[256,1024]{1,0:T(8,128)(2,1)}, bf16[256,1024]{1,0:T(8,128)(2,1)}, u32[]{:S(2)}, u32[]{:S(2)}) %collective-permute-start.91) | collective-permute-done | bytes 524320 | tf_op jit(solution)/shard_map/ppermute | solution.py:90
  855.0 8.6 collective-permute-done.103
  914.7 17.5 %collective-permute-start.99 = (bf16[1,2,1,2,1,32,768]{6,5,4,3,2,1,0:T(8,128)(2,1)}, bf16[1,2,1,2,1,32,768]{6,5,4,3,2,1,0:T(8,128)(2,1)}, u32[]{:S(2)}, u32[]{:S(2)}) collective-permute-start(bf16[1,2,1,2,1,32,768]{6,5,4,3,2,1,0:T(8,128)(2,1)} %dynamic-slice_convert_fusion.10), channel_id=1, source_target_pairs={{0,4},{1,5},{2,6},{3,7},{4,0},{5,1},{6,2},{7,3},{8,12},{9,13},{10,... | collective-permute-start | bytes 589832 | tf_op jit(solution)/shard_map/ppermute | solution.py:90
  (1267 shorter events, 595.1 us)
Async XLA Ops:
  49.4 43.6 %collective-permute-start.13 = (bf16[2,384,256]{2,1,0:T(8,128)(2,1)}, bf16[2,384,256]{2,1,0:T(8,128)(2,1)}, u32[]{:S(2)}, u32[]{:S(2)}) collective-permute-start(bf16[2,384,256]{2,1,0:T(8,128)(2,1)} %pad_maximum_fusion.57.refs_8_), channel_id=1, source_target_pairs={{0,1},{1,0},{2,3},{3,2},{4,5},{5,4},{6,7},{7,6},{8,9},{9,8},{10,11... | collective-permute-start | bytes 1179656 | tf_op jit(solution)/shard_map/ppermute | solution.py:90
  54.6 43.2 %collective-permute-start.1 = (bf16[2,384,256]{2,1,0:T(8,128)(2,1)}, bf16[2,384,256]{2,1,0:T(8,128)(2,1)}, u32[]{:S(2)}, u32[]{:S(2)}) collective-permute-start(bf16[2,384,256]{2,1,0:T(8,128)(2,1)} %pad_maximum_fusion.55), channel_id=1, source_target_pairs={{0,1},{1,0},{2,3},{3,2},{4,5},{5,4},{6,7},{7,6},{8,9},{9,8},{10,11... | collective-permute-start | bytes 1179656 | tf_op jit(solution)/shard_map/ppermute | solution.py:90
  54.6 38.8 %collective-permute-start.14 = (bf16[3,32,1024]{2,1,0:T(8,128)(2,1)}, bf16[3,32,1024]{2,1,0:T(8,128)(2,1)}, u32[]{:S(2)}, u32[]{:S(2)}) collective-permute-start(bf16[3,32,1024]{2,1,0:T(8,128)(2,1)} %param.20), channel_id=1, source_target_pairs={{0,0},{1,1},{2,4},{3,5},{4,16},{5,17},{6,20},{7,21},{8,2},{9,3},{1... | collective-permute-start | bytes 589832 | tf_op jit(solution)/shard_map/ppermute | solution.py:90
  58.7 53.9 %collective-permute-start.7 = (bf16[2,384,256]{2,1,0:T(8,128)(2,1)}, bf16[2,384,256]{2,1,0:T(8,128)(2,1)}, u32[]{:S(2)}, u32[]{:S(2)}) collective-permute-start(bf16[2,384,256]{2,1,0:T(8,128)(2,1)} %pad_maximum_fusion.56), channel_id=1, source_target_pairs={{0,16},{1,17},{2,18},{3,19},{4,20},{5,21},{6,22},{7,23},{8,24},{9,... | collective-permute-start | bytes 1179656 | tf_op jit(solution)/shard_map/ppermute | solution.py:90
  66.8 49.6 %all-to-all-start.2 = ((bf16[4,64,1024]{2,1,0:T(8,128)(2,1)}), bf16[4,64,1024]{2,1,0:T(8,128)(2,1)}, u32[]{:S(2)}, u32[]{:S(2)}) async-start(bf16[4,64,1024]{2,1,0:T(8,128)(2,1)} %reshape.729), calls=%async_computation.2 | async-start | bytes 1048576 | tf_op jit(solution)/shard_map/all_to_all | solution.py:156
  93.1 50.4 %collective-permute-start.29 = (bf16[256,1024]{1,0:T(8,128)(2,1)}, bf16[256,1024]{1,0:T(8,128)(2,1)}, u32[]{:S(2)}, u32[]{:S(2)}) collective-permute-start(bf16[256,1024]{1,0:T(8,128)(2,1)} %add_convert_fusion.3), channel_id=1, source_target_pairs={{0,8},{1,9},{2,10},{3,11},{4,12},{5,13},{6,14},{7,15},{8,0},{9,1},... | collective-permute-start | bytes 1572872 | tf_op jit(solution)/shard_map/ppermute | solution.py:90
  128.1 41.2 %collective-permute-start.19 = (bf16[1,256,1024]{2,1,0:T(8,128)(2,1)}, bf16[1,256,1024]{2,1,0:T(8,128)(2,1)}, u32[]{:S(2)}, u32[]{:S(2)}) collective-permute-start(bf16[1,256,1024]{2,1,0:T(8,128)(2,1)} %maximum_bitcast_fusion.1), channel_id=1, source_target_pairs={{0,4},{1,5},{2,6},{3,7},{4,0},{5,1},{6,2},{7,3},{8,12},{9,13},{10,... | collective-permute-start | bytes 1572872 | tf_op jit(solution)/shard_map/ppermute | solution.py:90
  130.6 49.9 %collective-permute-start.11 = (bf16[1,256,1024]{2,1,0:T(8,128)(2,1)}, bf16[1,256,1024]{2,1,0:T(8,128)(2,1)}, u32[]{:S(2)}, u32[]{:S(2)}) collective-permute-start(bf16[1,256,1024]{2,1,0:T(8,128)(2,1)} %maximum_bitcast_fusion.refs_8_), channel_id=1, source_target_pairs={{0,4},{1,5},{2,6},{3,7},{4,0},{5,1},{6,2},{7,3},{8,12},{9,13},{10,... | collective-permute-start | bytes 1572872 | tf_op jit(solution)/shard_map/ppermute | solution.py:90
  136.4 56.1 %collective-permute-start.17 = (bf16[4,96,1024]{2,1,0:T(8,128)(2,1)}, bf16[4,96,1024]{2,1,0:T(8,128)(2,1)}, u32[]{:S(2)}, u32[]{:S(2)}) collective-permute-start(bf16[4,96,1024]{2,1,0:T(8,128)(2,1)} %pad_maximum_fusion.47), channel_id=1, source_target_pairs={{0,1},{1,0},{2,3},{3,2},{4,5},{5,4},{6,7},{7,6},{8,9},{9,8},{10,11... | collective-permute-start | bytes 2359304 | tf_op jit(solution)/shard_map/ppermute | solution.py:90
  140.5 41.7 %collective-permute-start.3 = (bf16[128,1024]{1,0:T(8,128)(2,1)S(1)}, bf16[128,1024]{1,0:T(8,128)(2,1)S(1)}, u32[]{:S(2)}, u32[]{:S(2)}) collective-permute-start(bf16[128,1024]{1,0:T(8,128)(2,1)S(1)} %copy-done.200), channel_id=1, source_target_pairs={{0,0},{1,4},{2,2},{3,6},{4,8},{5,12},{6,10},{7,14},{8,1},{9,5},{10... | collective-permute-start | bytes 786440 | tf_op jit(solution)/shard_map/ppermute | solution.py:90
  143.5 40.8 %collective-permute-start.4 = (bf16[128,1024]{1,0:T(8,128)(2,1)S(1)}, bf16[128,1024]{1,0:T(8,128)(2,1)S(1)}, u32[]{:S(2)}, u32[]{:S(2)}) collective-permute-start(bf16[128,1024]{1,0:T(8,128)(2,1)S(1)} %copy-done.201), channel_id=1, source_target_pairs={{0,4},{1,0},{2,6},{3,2},{4,12},{5,8},{6,14},{7,10},{8,5},{9,1},{10... | collective-permute-start | bytes 786440 | tf_op jit(solution)/shard_map/ppermute | solution.py:90
  196.6 92.1 %collective-permute-start.24 = (bf16[4,384,256]{2,1,0:T(8,128)(2,1)}, bf16[4,384,256]{2,1,0:T(8,128)(2,1)}, u32[]{:S(2)}, u32[]{:S(2)}) collective-permute-start(bf16[4,384,256]{2,1,0:T(8,128)(2,1)} %pad_maximum_fusion.46.refs_8_), channel_id=1, source_target_pairs={{0,16},{1,17},{2,18},{3,19},{4,20},{5,21},{6,22},{7,23},{8,24},{9,... | collective-permute-start | bytes 2359304 | tf_op jit(solution)/shard_map/ppermute | solution.py:90
  199.6 36.1 %collective-permute-start.32 = (bf16[256,1024]{1,0:T(8,128)(2,1)}, bf16[256,1024]{1,0:T(8,128)(2,1)}, u32[]{:S(2)}, u32[]{:S(2)}) collective-permute-start(bf16[256,1024]{1,0:T(8,128)(2,1)} %slice.784), channel_id=1, source_target_pairs={{0,8},{1,9},{2,10},{3,11},{4,12},{5,13},{6,14},{7,15},{8,0},{9,1},... | collective-permute-start | bytes 1572872 | tf_op jit(solution)/shard_map/ppermute | solution.py:90
  211.2 54.4 %collective-permute-start.36 = (bf16[4,256,1024]{2,1,0:T(8,128)(2,1)S(1)}, bf16[4,256,1024]{2,1,0:T(8,128)(2,1)}, u32[]{:S(2)}, u32[]{:S(2)}) collective-permute-start(bf16[4,256,1024]{2,1,0:T(8,128)(2,1)S(1)} %pad_maximum_fusion.2.refs_7_), channel_id=1, source_target_pairs={{0,16},{1,17},{2,18},{3,19},{4,20},{5,21},{6,22},{7,23},{8,24},{9,... | collective-permute-start | bytes 6291464 | tf_op jit(solution)/shard_map/ppermute | solution.py:90
  239.3 50.8 %collective-permute-start.18 = (bf16[256,1024]{1,0:T(8,128)(2,1)S(1)}, bf16[256,1024]{1,0:T(8,128)(2,1)S(1)}, u32[]{:S(2)}, u32[]{:S(2)}) collective-permute-start(bf16[256,1024]{1,0:T(8,128)(2,1)S(1)} %slice.786), channel_id=1, source_target_pairs={{0,8},{1,9},{2,10},{3,11},{4,12},{5,13},{6,14},{7,15},{8,0},{9,1},... | collective-permute-start | bytes 1572872 | tf_op jit(solution)/shard_map/ppermute | solution.py:90
  239.4 37.9 %collective-permute-start.35 = (bf16[256,1024]{1,0:T(8,128)(2,1)S(1)}, bf16[256,1024]{1,0:T(8,128)(2,1)S(1)}, u32[]{:S(2)}, u32[]{:S(2)}) collective-permute-start(bf16[256,1024]{1,0:T(8,128)(2,1)S(1)} %add_convert_fusion.2), channel_id=1, source_target_pairs={{0,8},{1,9},{2,10},{3,11},{4,12},{5,13},{6,14},{7,15},{8,0},{9,1},... | collective-permute-start | bytes 1572872 | tf_op jit(solution)/shard_map/ppermute | solution.py:90
  252.4 37.7 %collective-permute-start.22 = (bf16[256,1024]{1,0:T(8,128)(2,1)}, bf16[256,1024]{1,0:T(8,128)(2,1)S(1)}, u32[]{:S(2)}, u32[]{:S(2)}) collective-permute-start(bf16[256,1024]{1,0:T(8,128)(2,1)} %fusion.86), channel_id=1, source_target_pairs={{0,2},{1,3},{2,0},{3,1},{4,6},{5,7},{6,4},{7,5},{8,10},{9,11},{10,... | collective-permute-start | bytes 1572872 | tf_op jit(solution)/shard_map/ppermute | solution.py:90
  318.2 57.1 %collective-permute-start.50 = (bf16[4,256,1024]{2,1,0:T(8,128)(2,1)}, bf16[4,256,1024]{2,1,0:T(8,128)(2,1)}, u32[]{:S(2)}, u32[]{:S(2)}) collective-permute-start(bf16[4,256,1024]{2,1,0:T(8,128)(2,1)} %pad_maximum_fusion.3.targets_0_), channel_id=1, source_target_pairs={{0,1},{1,0},{2,3},{3,2},{4,5},{5,4},{6,7},{7,6},{8,9},{9,8},{10,11... | collective-permute-start | bytes 6291464 | tf_op jit(solution)/shard_map/ppermute | solution.py:90
  548.4 47.8 %collective-permute-start.109 = (bf16[1,2,2,256,1024]{4,3,2,1,0:T(8,128)(2,1)S(1)}, bf16[1,2,2,256,1024]{4,3,2,1,0:T(8,128)(2,1)S(1)}, u32[]{:S(2)}, u32[]{:S(2)}) collective-permute-start(bf16[1,2,2,256,1024]{4,3,2,1,0:T(8,128)(2,1)S(1)} %fusion.24), channel_id=1, source_target_pairs={{0,16},{1,17},{2,18},{3,19},{4,20},{5,21},{6,22},{7,23},{8,24},{9,... | collective-permute-start | bytes 6291464 | tf_op jit(solution)/shard_map/ppermute | solution.py:90
  621.9 37.8 %collective-permute-start.69 = (bf16[256,1024]{1,0:T(8,128)(2,1)S(1)}, bf16[256,1024]{1,0:T(8,128)(2,1)S(1)}, u32[]{:S(2)}, u32[]{:S(2)}) collective-permute-start(bf16[256,1024]{1,0:T(8,128)(2,1)S(1)} %slice.772), channel_id=1, source_target_pairs={{0,8},{1,9},{2,10},{3,11},{4,12},{5,13},{6,14},{7,15},{8,0},{9,1},... | collective-permute-start | bytes 1572872 | tf_op jit(solution)/shard_map/ppermute | solution.py:90
  630.3 40.3 %collective-permute-start.111 = (bf16[1,1,1,256,1024]{4,3,2,1,0:T(8,128)(2,1)}, bf16[1,1,1,256,1024]{4,3,2,1,0:T(8,128)(2,1)}, u32[]{:S(2)}, u32[]{:S(2)}) collective-permute-start(bf16[1,1,1,256,1024]{4,3,2,1,0:T(8,128)(2,1)} %dynamic-slice_convert_fusion.2), channel_id=1, source_target_pairs={{0,4},{1,5},{2,6},{3,7},{4,0},{5,1},{6,2},{7,3},{8,12},{9,13},{10,... | collective-permute-start | bytes 1572872 | tf_op jit(solution)/shard_map/ppermute | solution.py:90
  661.9 62.6 %collective-permute-start.78 = (bf16[256,1024]{1,0:T(8,128)(2,1)}, bf16[256,1024]{1,0:T(8,128)(2,1)}, u32[]{:S(2)}, u32[]{:S(2)}) collective-permute-start(bf16[256,1024]{1,0:T(8,128)(2,1)} %get-tuple-element.209), channel_id=1, source_target_pairs={{0,2},{1,3},{2,0},{3,1},{4,6},{5,7},{6,4},{7,5},{8,10},{9,11},{10,... | collective-permute-start | bytes 1572872 | tf_op jit(solution)/shard_map/ppermute | solution.py:90
  674.3 50.7 %all-to-all-start.11 = ((bf16[4,32,1024]{2,1,0:T(8,128)(2,1)}), bf16[4,32,1024]{2,1,0:T(8,128)(2,1)}, u32[]{:S(2)}, u32[]{:S(2)}) async-start(bf16[4,32,1024]{2,1,0:T(8,128)(2,1)} %bitcast.277), calls=%async_computation.11 | async-start | bytes 524288 | tf_op jit(solution)/shard_map/all_to_all | solution.py:156
  711.2 75.1 %collective-permute-start.92 = (bf16[1,2,2,256,1024]{4,3,2,1,0:T(8,128)(2,1)}, bf16[1,2,2,256,1024]{4,3,2,1,0:T(8,128)(2,1)}, u32[]{:S(2)}, u32[]{:S(2)}) collective-permute-start(bf16[1,2,2,256,1024]{4,3,2,1,0:T(8,128)(2,1)} %fusion.26), channel_id=1, source_target_pairs={{0,16},{1,17},{2,18},{3,19},{4,20},{5,21},{6,22},{7,23},{8,24},{9,... | collective-permute-start | bytes 6291464 | tf_op jit(solution)/shard_map/ppermute | solution.py:90
  785.8 41.1 %collective-permute-start.90 = (bf16[256,1024]{1,0:T(8,128)(2,1)}, bf16[256,1024]{1,0:T(8,128)(2,1)}, u32[]{:S(2)}, u32[]{:S(2)}) collective-permute-start(bf16[256,1024]{1,0:T(8,128)(2,1)} %slice.765), channel_id=1, source_target_pairs={{0,8},{1,9},{2,10},{3,11},{4,12},{5,13},{6,14},{7,15},{8,0},{9,1},... | collective-permute-start | bytes 1572872 | tf_op jit(solution)/shard_map/ppermute | solution.py:90
  790.5 87.9 %collective-permute-start.107 = (bf16[1,2,1,256,1024]{4,3,2,1,0:T(8,128)(2,1)}, bf16[1,2,1,256,1024]{4,3,2,1,0:T(8,128)(2,1)}, u32[]{:S(2)}, u32[]{:S(2)}) collective-permute-start(bf16[1,2,1,256,1024]{4,3,2,1,0:T(8,128)(2,1)} %dynamic-slice_convert_fusion.1.refs_2_), channel_id=1, source_target_pairs={{0,1},{1,0},{2,3},{3,2},{4,5},{5,4},{6,7},{7,6},{8,9},{9,8},{10,11... | collective-permute-start | bytes 3145736 | tf_op jit(solution)/shard_map/ppermute | solution.py:90
  819.1 65.7 %collective-permute-start.83 = (bf16[256,1024]{1,0:T(8,128)(2,1)}, bf16[256,1024]{1,0:T(8,128)(2,1)}, u32[]{:S(2)}, u32[]{:S(2)}) collective-permute-start(bf16[256,1024]{1,0:T(8,128)(2,1)} %slice.768), channel_id=1, source_target_pairs={{0,8},{1,9},{2,10},{3,11},{4,12},{5,13},{6,14},{7,15},{8,0},{9,1},... | collective-permute-start | bytes 1572872 | tf_op jit(solution)/shard_map/ppermute | solution.py:90
  882.3 79.0 %collective-permute-start.108 = (bf16[1,1,1,256,1024]{4,3,2,1,0:T(8,128)(2,1)}, bf16[1,1,1,256,1024]{4,3,2,1,0:T(8,128)(2,1)}, u32[]{:S(2)}, u32[]{:S(2)}) collective-permute-start(bf16[1,1,1,256,1024]{4,3,2,1,0:T(8,128)(2,1)} %dynamic-slice_convert_fusion.3), channel_id=1, source_target_pairs={{0,4},{1,5},{2,6},{3,7},{4,0},{5,1},{6,2},{7,3},{8,12},{9,13},{10,... | collective-permute-start | bytes 1572872 | tf_op jit(solution)/shard_map/ppermute | solution.py:90
  897.5 34.8 %collective-permute-start.88 = (bf16[128,1024]{1,0:T(8,128)(2,1)}, bf16[128,1024]{1,0:T(8,128)(2,1)}, u32[]{:S(2)}, u32[]{:S(2)}) collective-permute-start(bf16[128,1024]{1,0:T(8,128)(2,1)} %get-tuple-element.241), channel_id=1, source_target_pairs={{0,1},{1,9},{2,3},{3,11},{4,0},{5,8},{6,2},{7,10},{8,5},{9,13},{10... | collective-permute-start | bytes 786440 | tf_op jit(solution)/shard_map/ppermute | solution.py:90
  902.2 36.6 %all-to-all-start.12 = ((f32[32,1,576]{2,1,0:T(1,128)}), f32[32,1,576]{2,1,0:T(1,128)S(1)}, u32[]{:S(2)}, u32[]{:S(2)}) async-start(f32[32,1,576]{2,1,0:T(1,128)} %reshape.801), calls=%async_computation.12 | async-start | bytes 163840 | tf_op jit(solution)/shard_map/all_to_all | solution.py:1071
  911.6 46.1 %collective-permute-start.105 = (bf16[1,1,1,96,1024]{4,3,2,1,0:T(8,128)(2,1)}, bf16[1,1,1,96,1024]{4,3,2,1,0:T(8,128)(2,1)}, u32[]{:S(2)}, u32[]{:S(2)}) collective-permute-start(bf16[1,1,1,96,1024]{4,3,2,1,0:T(8,128)(2,1)} %dynamic-slice_convert_fusion.8), channel_id=1, source_target_pairs={{0,4},{1,5},{2,6},{3,7},{4,0},{5,1},{6,2},{7,3},{8,12},{9,13},{10,... | collective-permute-start | bytes 589832 | tf_op jit(solution)/shard_map/ppermute | solution.py:90
  914.7 34.8 %collective-permute-start.99 = (bf16[1,2,1,2,1,32,768]{6,5,4,3,2,1,0:T(8,128)(2,1)}, bf16[1,2,1,2,1,32,768]{6,5,4,3,2,1,0:T(8,128)(2,1)}, u32[]{:S(2)}, u32[]{:S(2)}) collective-permute-start(bf16[1,2,1,2,1,32,768]{6,5,4,3,2,1,0:T(8,128)(2,1)} %dynamic-slice_convert_fusion.10), channel_id=1, source_target_pairs={{0,4},{1,5},{2,6},{3,7},{4,0},{5,1},{6,2},{7,3},{8,12},{9,13},{10,... | collective-permute-start | bytes 589832 | tf_op jit(solution)/shard_map/ppermute | solution.py:90
  (400 other events, 5126.9 us)
